TPU v7x, 32 devices: a whole 2x2x4 slice. The times are simulated.
32 devices in a mesh: shot: 8 (over z, x), sub: 4 (over y, core).
Axes of the slice: x: 2, y: 2, z: 4, core: 2. Of those that a mesh axis runs over, the one named last changes fastest.
Arguments:
- stiffness: float32 [64, 32, 384], P('sub'), may hold values from 0.04 to 0.15
- buoyancy_first: float32 [64, 32, 384], P('sub'), may hold values from 0.6 to 1.3
- buoyancy_second: float32 [64, 32, 384], P('sub'), may hold values from 0.6 to 1.3
- buoyancy_third: float32 [64, 32, 384], P('sub'), may hold values from 0.6 to 1.3
- adjoint_before: float32 [8, 64, 32, 384], P('shot', 'sub'), may hold values from -6 to 6
- adjoint_current: float32 [8, 64, 32, 384], P('shot', 'sub'), may hold values from -6 to 6
- forward_field: bfloat16 [8, 8, 64, 32, 384], P('shot', None, 'sub'), may hold values from -6 to 6
- traces: float32 [16384, 256], P(('shot', 'sub')), may hold values from -6 to 6
- receiver_target: int32 [16384, 1], P(('shot', 'sub')), may hold values from 0 to 31; in each aligned block of 512 rows (0 to 511, 512 to 1023, ...) at most 24 rows name the same one
- receiver_cell: int32 [16384], P(('shot', 'sub')), may hold values from 0 to 196607
- source_cell: int32 [8, 3], P('shot'), may hold values from 0 to 31
Outputs:
- gradient: float32 [64, 12288], P('sub', 'shot')
- adjoint_earlier: float32 [8, 64, 32, 384], P('shot', 'sub')
- adjoint_latest: float32 [8, 64, 32, 384], P('shot', 'sub')
Inputs may be any that keep to these rules, and one draw needn't show every extreme that they name: `receiver_target`: at most 24 of the receivers stored on one device share a value, and 24 is reached. `receiver_cell`: flattened with the first dimension slowest.
All inputs are finite; a program needn't handle non-finite values.
Results may differ from a plain program's by a relative error of at most 0.0003.
Values sent between devices are 32-bit elements; how exact they have to be, the bound alone decides.
A program may use at most 128 MiB of HBM per device.

v0:
```python
import jax
import jax.numpy as jnp
from jax import lax
from jax.sharding import PartitionSpec as P

MUTE = 6


COEFFS = (1225.0 / 1024.0, -245.0 / 3072.0, 49.0 / 5120.0, -5.0 / 7168.0)
DAMP = 0.1


def padded(cells, sides, width):
    for axis, dim in sides:
        count = lax.axis_size(axis)
        ends = count - 1
        head = lax.slice_in_dim(cells, 0, width, axis=dim)
        tail = lax.slice_in_dim(cells, cells.shape[dim] - width, cells.shape[dim], axis=dim)
        cells = jnp.concatenate(
            [
                lax.ppermute(tail, axis, [(i, (i + 1) % count) for i in range(ends)]),
                cells,
                lax.ppermute(head, axis, [((i + 1) % count, i) for i in range(ends)]),
            ],
            axis=dim,
        )
    return cells


def take_slice(extended, dimension, offset, length):
    return lax.slice_in_dim(extended, offset, offset + length, axis=dimension)


def forward_difference(extended, dimension, offset, length):
    summed = COEFFS[0] * (
        take_slice(extended, dimension, offset + 1, length)
        - take_slice(extended, dimension, offset, length)
    )
    for order in range(2, 5):
        summed = summed + COEFFS[order - 1] * (
            take_slice(extended, dimension, offset + order, length)
            - take_slice(extended, dimension, offset + 1 - order, length)
        )
    return summed


def backward_difference(extended, dimension, offset, length):
    summed = COEFFS[0] * (
        take_slice(extended, dimension, offset, length)
        - take_slice(extended, dimension, offset - 1, length)
    )
    for order in range(2, 5):
        summed = summed + COEFFS[order - 1] * (
            take_slice(extended, dimension, offset + order - 1, length)
            - take_slice(extended, dimension, offset - order, length)
        )
    return summed


def pad_along(wave_field, dimension, amount):
    widths = [(0, 0)] * wave_field.ndim
    widths[dimension] = (amount, amount)
    return jnp.pad(wave_field, widths)


def local_divergence(wave_field, buoyancy, dimension):
    length = wave_field.shape[dimension]
    flux_field = buoyancy * forward_difference(
        pad_along(wave_field, dimension, 4), dimension, 4, length
    )
    return backward_difference(pad_along(flux_field, dimension, 4), dimension, 4, length)


def trace_kernel(sample_count, step_count):
    sample_pos = jnp.arange(sample_count, dtype=jnp.float32)[:, None]
    centers = (jnp.arange(step_count, dtype=jnp.float32)[None, :] + 0.5) * (
        sample_count / step_count
    )
    return 0.25 * jnp.exp(-jnp.abs(sample_pos - centers) / (sample_count / 8.0))


def first_divergence(current, buoyancy_first):
    slab_depth = current.shape[0]
    extended = padded(current, (("sub", 0),), 4)
    flux_field = buoyancy_first * forward_difference(extended, 0, 4, slab_depth)
    flux_wide = padded(flux_field, (("sub", 0),), 4)
    return backward_difference(flux_wide, 0, 4, slab_depth)


def local(
    stiffness,
    buoyancy_first,
    buoyancy_second,
    buoyancy_third,
    adjoint_before,
    adjoint_current,
    forward_field,
    traces,
    receiver_target,
    receiver_cell,
    source_cell,
):
    device_count = lax.axis_size(("shot", "sub"))
    sample_count = traces.shape[1]
    step_count = forward_field.shape[1]
    slab_depth = stiffness.shape[0]
    row_count = traces.shape[0]
    capacity = max(2, (3 * row_count + 2 * device_count - 1) // (2 * device_count))
    kernel = trace_kernel(sample_count, step_count)
    target = receiver_target[:, 0]
    onehot = target[:, None] == jnp.arange(device_count, dtype=jnp.int32)[None, :]
    row_ids = jnp.arange(row_count, dtype=jnp.int32)
    lower = (row_ids[:, None] >= row_ids[None, :]).astype(jnp.bfloat16)
    running = jnp.dot(lower, onehot.astype(jnp.bfloat16), preferred_element_type=jnp.float32)
    slot_index = (jnp.sum(jnp.where(onehot, running, jnp.float32(0.0)), axis=1) - 1.0).astype(
        jnp.int32
    )
    place_buffer = (
        jnp.zeros((device_count, capacity), jnp.float32)
        .at[target, slot_index]
        .set(receiver_cell.astype(jnp.float32))
    )
    row_buffer = (
        jnp.zeros((device_count, capacity, sample_count), jnp.float32)
        .at[target, slot_index]
        .set(traces)
    )
    got_rows, got_places = (
        lax.all_to_all(row_buffer, ("shot", "sub"), split_axis=0, concat_axis=0, tiled=True),
        lax.all_to_all(place_buffer, ("shot", "sub"), split_axis=0, concat_axis=0, tiled=True),
    )
    received = jnp.dot(
        got_rows.reshape(-1, sample_count),
        kernel,
        precision=lax.Precision.HIGHEST,
        preferred_element_type=jnp.float32,
    )
    place_index = got_places.reshape(-1).astype(jnp.int32)
    step_values = received.T
    earlier = adjoint_before[0]
    current = adjoint_current[0]
    forward_now = forward_field[0]
    image_sum = jnp.zeros(current.shape, jnp.float32)
    illumination = jnp.zeros(current.shape, jnp.float32)
    for moment in range(step_count):
        divergence = first_divergence(current, buoyancy_first)
        divergence = divergence + local_divergence(current, buoyancy_second, 1)
        divergence = divergence + local_divergence(current, buoyancy_third, 2)
        change = (
            (stiffness * divergence)
            .reshape(-1)
            .at[place_index]
            .add(step_values[moment])
            .reshape(current.shape)
        )
        following = 2.0 * current - earlier + change
        frame = forward_now[moment].astype(jnp.float32)
        image_sum = image_sum + frame * change
        illumination = illumination + frame * frame
        earlier, current = (current, following)
    source_pos = source_cell[0].astype(jnp.float32)
    coord_first = (
        lax.axis_index("sub") * slab_depth + jnp.arange(slab_depth, dtype=jnp.int32)
    ).astype(jnp.float32)[:, None, None]
    coord_second = jnp.arange(current.shape[1], dtype=jnp.float32)[None, :, None]
    coord_third = jnp.arange(current.shape[2], dtype=jnp.float32)[None, None, :]
    distance = (
        (coord_first - source_pos[0]) ** 2
        + (coord_second - source_pos[1]) ** 2
        + (coord_third - source_pos[2]) ** 2
    )
    mute_weight = 1.0 - jnp.exp(-distance / (2.0 * MUTE * MUTE))
    muted_image = (mute_weight * image_sum).reshape(slab_depth, -1)
    flat_light = illumination.reshape(slab_depth, -1)
    summed_image, summed_light = (
        lax.psum_scatter(muted_image, "shot", scatter_dimension=1, tiled=True),
        lax.psum_scatter(flat_light, "shot", scatter_dimension=1, tiled=True),
    )
    gradient = summed_image / (summed_light / (step_count * lax.axis_size("shot")) + DAMP)
    return (gradient, earlier[None], current[None])


def solution(mesh):
    placed = (
        P("sub", None, None),
        P("sub", None, None),
        P("sub", None, None),
        P("sub", None, None),
        P("shot", "sub", None, None),
        P("shot", "sub", None, None),
        P("shot", None, "sub", None, None),
        P(("shot", "sub"), None),
        P(("shot", "sub"), None),
        P(("shot", "sub")),
        P("shot", None),
    )
    return jax.shard_map(
        local,
        mesh=mesh,
        in_specs=placed,
        out_specs=(P("sub", "shot"), P("shot", "sub", None, None), P("shot", "sub", None, None)),
        check_vma=False,
    )
```

profile of v0, /device:TPU:0, one launch (start us, length us, event | category | flops | bytes accessed | tf_op | source)
XLA Modules:
  0.0 600.3 jit_solution(12767653280299580792)
XLA Ops:
  10.2 3.0 collective-permute-start.1
  15.7 25.1 %scatter_fusion = f32[32,24]{0,1:T(8,128)S(1)} fusion(f32[32,24]{0,1:T(8,128)S(1)} %broadcast_in_dim.7, s32[512]{0:T(512)S(1)} %bitcast.47, f32[512]{0:T(512)S(1)} %convert_element_type.146), kind=kCustom, calls=%fused_computation | custom fusion | bytes 10240 | tf_op jit(solution)/shard_map/scatter | solution.py:121
  41.5 7.3 %all-to-all-start = ((f32[32,1,24]{2,1,0:T(1,128)}), f32[32,1,24]{2,1,0:T(1,128)S(1)}, u32[]{:S(2)}, u32[]{:S(2)}) async-start(f32[32,1,24]{2,1,0:T(1,128)} %copy.16), calls=%async_computation | async-start | bytes 32768 | tf_op jit(solution)/shard_map/all_to_all | solution.py:130
  49.8 56.9 %scatter_fusion.1 = f32[32,24,256]{2,1,0:T(8,128)} fusion(f32[32,24,256]{2,1,0:T(8,128)} %broadcast_in_dim.10, s32[512]{0:T(512)S(1)} %bitcast.48, f32[512,256]{1,0:T(8,128)S(1)} %copy-done.49), kind=kCustom, calls=%fused_computation.1 | custom fusion | bytes 1576960 | tf_op jit(solution)/shard_map/scatter | solution.py:126
  106.7 5.8 all-to-all-start.1
  112.6 12.4 %fusion.446 = (f32[16,32,384]{2,1,0:T(8,128)}, f32[16,32,384]{2,1,0:T(8,128)S(1)}, f32[16,32,384]{2,1,0:T(8,128)}) fusion(f32[16,32,384]{2,1,0:T(8,128)S(1)} %copy-done.4, f32[16,32,384]{2,1,0:T(8,128)} %bitcast.49, f32[16,32,384]{2,1,0:T(8,128)S(1)} %copy-done.9, f32[4,32,384]{2,1,0:T(8,128)S(1)} %collective-permute-done.1, ...), kind=kLoop, calls=%fused_computation.842 | loop fusion | flops 8454144 | bytes 5898240 | tf_op jit(solution)/shard_map/mul | solution.py:68
  133.4 10.7 %fusion.162 = f32[16,32,384]{2,1,0:T(8,128)} fusion(f32[16,32,384]{2,1,0:T(8,128)S(1)} %copy-done.22, f32[16,32,384]{2,1,0:T(8,128)} %copy-done.37, f32[16,32,384]{2,1,0:T(8,128)} %get-tuple-element.78, f32[4,32,384]{2,1,0:T(8,128)S(1)} %collective-permute-done.3, f32[16,32,384]{2,1,0:T(8,128)} %get-tuple-element.76, ...), kind=kLoop, calls=%fused_computation.558 | loop fusion | flops 8454144 | bytes 4325376 | tf_op jit(solution)/shard_map/mul | solution.py:150
  147.3 5.3 scatter_fusion.2
  156.8 6.8 %collective-permute-start.5 = (f32[4,32,384]{2,1,0:T(8,128)S(1)}, f32[4,32,384]{2,1,0:T(8,128)S(1)}, u32[]{:S(2)}, u32[]{:S(2)}) collective-permute-start(f32[4,32,384]{2,1,0:T(8,128)S(1)} %get-tuple-element.73), channel_id=1, source_target_pairs={{0,1},{1,2},{2,3},{4,5},{5,6},{6,7},{8,9},{9,10},{10,11},{12,13},{... | collective-permute-start | bytes 589832 | tf_op jit(solution)/shard_map/ppermute | solution.py:21
  167.3 5.2 collective-permute-start.6
  173.9 4.0 collective-permute-done.7
  177.9 3.2 fusion.140
  182.3 5.5 scatter_fusion.3
  192.1 6.8 %collective-permute-start.9 = (f32[4,32,384]{2,1,0:T(8,128)S(1)}, f32[4,32,384]{2,1,0:T(8,128)S(1)}, u32[]{:S(2)}, u32[]{:S(2)}) collective-permute-start(f32[4,32,384]{2,1,0:T(8,128)S(1)} %get-tuple-element.66), channel_id=1, source_target_pairs={{0,1},{1,2},{2,3},{4,5},{5,6},{6,7},{8,9},{9,10},{10,11},{12,13},{... | collective-permute-start | bytes 589832 | tf_op jit(solution)/shard_map/ppermute | solution.py:21
  202.6 5.2 collective-permute-start.10
  209.1 4.0 collective-permute-done.11
  213.1 3.2 fusion.118
  217.5 5.3 scatter_fusion.4
  227.2 6.8 %collective-permute-start.13 = (f32[4,32,384]{2,1,0:T(8,128)S(1)}, f32[4,32,384]{2,1,0:T(8,128)S(1)}, u32[]{:S(2)}, u32[]{:S(2)}) collective-permute-start(f32[4,32,384]{2,1,0:T(8,128)S(1)} %get-tuple-element.59), channel_id=1, source_target_pairs={{0,1},{1,2},{2,3},{4,5},{5,6},{6,7},{8,9},{9,10},{10,11},{12,13},{... | collective-permute-start | bytes 589832 | tf_op jit(solution)/shard_map/ppermute | solution.py:21
  237.7 5.2 collective-permute-start.14
  244.2 4.0 collective-permute-done.15
  248.2 3.2 fusion.96
  252.6 5.3 scatter_fusion.5
  262.3 7.3 %collective-permute-start.17 = (f32[4,32,384]{2,1,0:T(8,128)S(1)}, f32[4,32,384]{2,1,0:T(8,128)S(1)}, u32[]{:S(2)}, u32[]{:S(2)}) collective-permute-start(f32[4,32,384]{2,1,0:T(8,128)S(1)} %get-tuple-element.52), channel_id=1, source_target_pairs={{0,1},{1,2},{2,3},{4,5},{5,6},{6,7},{8,9},{9,10},{10,11},{12,13},{... | collective-permute-start | bytes 589832 | tf_op jit(solution)/shard_map/ppermute | solution.py:21
  272.8 5.2 collective-permute-start.18
  279.3 4.0 collective-permute-done.19
  283.4 3.2 fusion.74
  288.7 6.7 %scatter_fusion.6 = f32[196608]{0:T(1024)} fusion(f32[196608]{0:T(1024)} %reshape.292, s32[768]{0:T(1024)S(1)} %fusion.670, f32[768]{0:T(1024)S(1)} %get-tuple-element.6), kind=kCustom, calls=%fused_computation.6 | custom fusion | flops 768 | bytes 12288 | tf_op jit(solution)/shard_map/scatter-add | solution.py:153
  300.9 6.9 %collective-permute-start.21 = (f32[4,32,384]{2,1,0:T(8,128)S(1)}, f32[4,32,384]{2,1,0:T(8,128)S(1)}, u32[]{:S(2)}, u32[]{:S(2)}) collective-permute-start(f32[4,32,384]{2,1,0:T(8,128)S(1)} %get-tuple-element.45), channel_id=1, source_target_pairs={{0,1},{1,2},{2,3},{4,5},{5,6},{6,7},{8,9},{9,10},{10,11},{12,13},{... | collective-permute-start | bytes 589832 | tf_op jit(solution)/shard_map/ppermute | solution.py:21
  311.4 5.2 collective-permute-start.22
  318.0 4.0 collective-permute-done.23
  322.0 3.2 fusion.52
  327.3 6.7 %scatter_fusion.7 = f32[196608]{0:T(1024)} fusion(f32[196608]{0:T(1024)} %reshape.295, s32[768]{0:T(1024)S(1)} %fusion.670, f32[768]{0:T(1024)S(1)} %get-tuple-element.5), kind=kCustom, calls=%fused_computation.7 | custom fusion | flops 768 | bytes 12288 | tf_op jit(solution)/shard_map/scatter-add | solution.py:153
  339.5 7.0 %collective-permute-start.25 = (f32[4,32,384]{2,1,0:T(8,128)S(1)}, f32[4,32,384]{2,1,0:T(8,128)S(1)}, u32[]{:S(2)}, u32[]{:S(2)}) collective-permute-start(f32[4,32,384]{2,1,0:T(8,128)S(1)} %get-tuple-element.38), channel_id=1, source_target_pairs={{0,1},{1,2},{2,3},{4,5},{5,6},{6,7},{8,9},{9,10},{10,11},{12,13},{... | collective-permute-start | bytes 589832 | tf_op jit(solution)/shard_map/ppermute | solution.py:21
  347.5 3.5 fusion.584
  351.9 5.2 collective-permute-start.26
  362.6 10.8 %fusion.30 = f32[16,32,384]{2,1,0:T(8,128)} fusion(f32[16,32,384]{2,1,0:T(8,128)} %param.11, f32[16,32,384]{2,1,0:T(8,128)} %copy-done.36, f32[16,32,384]{2,1,0:T(8,128)} %get-tuple-element.35, f32[4,32,384]{2,1,0:T(8,128)S(1)} %collective-permute-done.27, f32[16,32,384]{2,1,0:T(8,128)} %get-tuple-element.34, f32[4,32,384]{2,1,0:T(8,128)S(1)} %collective-permute-done.26), kind=kLoop, calls=%fused_computation.426 | loop fusion | flops 8454144 | bytes 4325376 | tf_op jit(solution)/shard_map/mul | solution.py:150
  375.4 6.7 %scatter_fusion.8 = f32[196608]{0:T(1024)} fusion(f32[196608]{0:T(1024)} %reshape.298, s32[768]{0:T(1024)S(1)} %fusion.670, f32[768]{0:T(1024)S(1)} %get-tuple-element.4), kind=kCustom, calls=%fused_computation.8 | custom fusion | flops 768 | bytes 12288 | tf_op jit(solution)/shard_map/scatter-add | solution.py:153
  387.6 6.7 %collective-permute-start.29 = (f32[4,32,384]{2,1,0:T(8,128)S(1)}, f32[4,32,384]{2,1,0:T(8,128)S(1)}, u32[]{:S(2)}, u32[]{:S(2)}) collective-permute-start(f32[4,32,384]{2,1,0:T(8,128)S(1)} %get-tuple-element.31), channel_id=1, source_target_pairs={{0,1},{1,2},{2,3},{4,5},{5,6},{6,7},{8,9},{9,10},{10,11},{12,13},{... | collective-permute-start | bytes 589832 | tf_op jit(solution)/shard_map/ppermute | solution.py:21
  395.6 3.6 fusion.607
  400.0 5.1 collective-permute-start.30
  432.2 10.9 %fusion.8 = f32[16,32,384]{2,1,0:T(8,128)} fusion(f32[16,32,384]{2,1,0:T(8,128)} %param.11, f32[16,32,384]{2,1,0:T(8,128)} %copy-done.35, f32[16,32,384]{2,1,0:T(8,128)} %get-tuple-element.29, f32[4,32,384]{2,1,0:T(8,128)S(1)} %collective-permute-done.31, f32[16,32,384]{2,1,0:T(8,128)} %get-tuple-element.27, f32[4,32,384]{2,1,0:T(8,128)S(1)} %collective-permute-done.30), kind=kLoop, calls=%fused_computation.404 | loop fusion | flops 8454144 | bytes 4325376 | tf_op jit(solution)/shard_map/mul | solution.py:150
  445.2 6.7 %scatter_fusion.9 = f32[196608]{0:T(1024)} fusion(f32[196608]{0:T(1024)} %reshape.301, s32[768]{0:T(1024)S(1)} %fusion.670, f32[768]{0:T(1024)S(1)} %get-tuple-element.3), kind=kCustom, calls=%fused_computation.9 | custom fusion | flops 768 | bytes 12288 | tf_op jit(solution)/shard_map/scatter-add | solution.py:153
  454.1 6.9 %multiply_add_fusion = (f32[16,12288]{1,0:T(8,128)}, f32[16,12288]{1,0:T(8,128)}) fusion(f32[16,12288]{1,0:T(8,128)} %bitcast.57, f32[16,12288]{1,0:T(8,128)} %bitcast.56, f32[16,12288]{1,0:T(8,128)} %bitcast.55, f32[16,12288]{1,0:T(8,128)} %bitcast.54, f32[16,12288]{1,0:T(8,128)} %bitcast.53, f32[16,12288]{1,0:T(8,128)} %bitcast.52, ...), kind=kLoop, calls=%fused_computation.1095 | loop fusion | flops 6881280 | bytes 14991360 | tf_op jit(solution)/shard_map/add | solution.py:159
  466.1 3.8 subtract_add_fusion.4
  473.4 3.2 subtract_add_fusion
  476.6 50.0 %reduce-scatter.3.cloned.1.call-done = f32[16,1536]{1,0:T(8,128)} async-done(((f32[16,12288]{1,0:T(8,128)}), f32[16,1536]{1,0:T(8,128)}) %reduce-scatter.3.cloned.1.call-update) | async-done | bytes 98320 | tf_op jit(solution)/shard_map/reduce_scatter | solution.py:176
  526.6 65.0 %reduce-scatter.5.cloned.1.call-done = f32[16,1536]{1,0:T(8,128)} async-done(((f32[16,12288]{1,0:T(8,128)}), f32[16,1536]{1,0:T(8,128)}) %reduce-scatter.5.cloned.1.call-update) | async-done | bytes 98320 | tf_op jit(solution)/shard_map/reduce_scatter | solution.py:177
  (250 shorter events, 136.9 us)
Async XLA Ops:
  7.2 42.7 %copy-start.49 = (f32[512,256]{1,0:T(8,128)S(1)}, f32[512,256]{1,0:T(8,128)}, u32[]{:S(2)}) copy-start(f32[512,256]{1,0:T(8,128)} %param.18) | copy-start | bytes 1572868
  9.0 103.6 %collective-permute-start = (f32[4,32,384]{2,1,0:T(8,128)}, f32[4,32,384]{2,1,0:T(8,128)S(1)}, u32[]{:S(2)}, u32[]{:S(2)}) collective-permute-start(f32[4,32,384]{2,1,0:T(8,128)} %get-tuple-element.79), channel_id=1, source_target_pairs={{1,0},{2,1},{3,2},{5,4},{6,5},{7,6},{9,8},{10,9},{11,10},{13,12},{... | collective-permute-start | bytes 589832 | tf_op jit(solution)/shard_map/ppermute | solution.py:23
  10.2 102.3 %collective-permute-start.1 = (f32[4,32,384]{2,1,0:T(8,128)S(1)}, f32[4,32,384]{2,1,0:T(8,128)S(1)}, u32[]{:S(2)}, u32[]{:S(2)}) collective-permute-start(f32[4,32,384]{2,1,0:T(8,128)S(1)} %get-tuple-element.80), channel_id=1, source_target_pairs={{0,1},{1,2},{2,3},{4,5},{5,6},{6,7},{8,9},{9,10},{10,11},{12,13},{... | collective-permute-start | bytes 589832 | tf_op jit(solution)/shard_map/ppermute | solution.py:21
  41.5 65.2 %all-to-all-start = ((f32[32,1,24]{2,1,0:T(1,128)}), f32[32,1,24]{2,1,0:T(1,128)S(1)}, u32[]{:S(2)}, u32[]{:S(2)}) async-start(f32[32,1,24]{2,1,0:T(1,128)} %copy.16), calls=%async_computation | async-start | bytes 32768 | tf_op jit(solution)/shard_map/all_to_all | solution.py:130
  49.8 62.7 %copy-start.4 = (f32[16,32,384]{2,1,0:T(8,128)S(1)}, f32[16,32,384]{2,1,0:T(8,128)}, u32[]{:S(2)}) copy-start(f32[16,32,384]{2,1,0:T(8,128)} %param.14) | copy-start | bytes 2359300
  49.8 62.8 %copy-start.9 = (f32[16,32,384]{2,1,0:T(8,128)S(1)}, f32[16,32,384]{2,1,0:T(8,128)}, u32[]{:S(2)}) copy-start(f32[16,32,384]{2,1,0:T(8,128)} %param.12) | copy-start | bytes 2359300
  49.8 62.8 %copy-start.15 = (f32[16,32,384]{2,1,0:T(8,128)S(1)}, f32[16,32,384]{2,1,0:T(8,128)}, u32[]{:S(2)}) copy-start(f32[16,32,384]{2,1,0:T(8,128)} %param.13) | copy-start | bytes 2359300
  106.7 38.6 %all-to-all-start.1 = ((f32[32,24,256]{2,1,0:T(8,128)}), f32[32,24,256]{2,1,0:T(8,128)}, u32[]{:S(2)}, u32[]{:S(2)}) async-start(f32[32,24,256]{2,1,0:T(8,128)} %scatter_fusion.1), calls=%async_computation.1 | async-start | bytes 1572864 | tf_op jit(solution)/shard_map/all_to_all | solution.py:129
  112.5 414.1 %reduce-scatter.3.cloned.1.call-start = ((), (), s32[]{:S(2)}) async-start(), calls=%async_computation.4 | async-start | bytes 884736 | tf_op jit(solution)/shard_map/reduce_scatter | solution.py:176
  112.6 17.5 %copy-start.52 = (f32[32,1,24]{2,1,0:T(1,128)S(1)}, f32[32,1,24]{2,1,0:T(1,128)}, u32[]{:S(2)}) copy-start(f32[32,1,24]{2,1,0:T(1,128)} %copy-done.51) | copy-start | bytes 9220
  112.6 20.8 %copy-start.22 = (f32[16,32,384]{2,1,0:T(8,128)S(1)}, f32[16,32,384]{2,1,0:T(8,128)}, u32[]{:S(2)}) copy-start(f32[16,32,384]{2,1,0:T(8,128)} %param.11) | copy-start | bytes 2359300
  126.7 4.9 collective-permute-start.2
  128.7 4.7 collective-permute-start.3
  155.5 8.2 %collective-permute-start.4 = (f32[4,32,384]{2,1,0:T(8,128)S(1)}, f32[4,32,384]{2,1,0:T(8,128)S(1)}, u32[]{:S(2)}, u32[]{:S(2)}) collective-permute-start(f32[4,32,384]{2,1,0:T(8,128)S(1)} %get-tuple-element.72), channel_id=1, source_target_pairs={{1,0},{2,1},{3,2},{5,4},{6,5},{7,6},{9,8},{10,9},{11,10},{13,12},{... | collective-permute-start | bytes 589832 | tf_op jit(solution)/shard_map/ppermute | solution.py:23
  156.8 21.0 %copy-start.23 = (f32[16,32,384]{2,1,0:T(8,128)S(1)}, f32[16,32,384]{2,1,0:T(8,128)}, u32[]{:S(2)}) copy-start(f32[16,32,384]{2,1,0:T(8,128)} %param.11) | copy-start | bytes 2359300
  156.8 7.9 %collective-permute-start.5 = (f32[4,32,384]{2,1,0:T(8,128)S(1)}, f32[4,32,384]{2,1,0:T(8,128)S(1)}, u32[]{:S(2)}, u32[]{:S(2)}) collective-permute-start(f32[4,32,384]{2,1,0:T(8,128)S(1)} %get-tuple-element.73), channel_id=1, source_target_pairs={{0,1},{1,2},{2,3},{4,5},{5,6},{6,7},{8,9},{9,10},{10,11},{12,13},{... | collective-permute-start | bytes 589832 | tf_op jit(solution)/shard_map/ppermute | solution.py:21
  167.3 6.5 %collective-permute-start.6 = (f32[4,32,384]{2,1,0:T(8,128)S(1)}, f32[4,32,384]{2,1,0:T(8,128)S(1)}, u32[]{:S(2)}, u32[]{:S(2)}) collective-permute-start(f32[4,32,384]{2,1,0:T(8,128)S(1)} %get-tuple-element.67), channel_id=1, source_target_pairs={{0,1},{1,2},{2,3},{4,5},{5,6},{6,7},{8,9},{9,10},{10,11},{12,13},{... | collective-permute-start | bytes 589832 | tf_op jit(solution)/shard_map/ppermute | solution.py:21
  172.5 5.3 collective-permute-start.7
  190.7 8.2 %collective-permute-start.8 = (f32[4,32,384]{2,1,0:T(8,128)S(1)}, f32[4,32,384]{2,1,0:T(8,128)S(1)}, u32[]{:S(2)}, u32[]{:S(2)}) collective-permute-start(f32[4,32,384]{2,1,0:T(8,128)S(1)} %get-tuple-element.65), channel_id=1, source_target_pairs={{1,0},{2,1},{3,2},{5,4},{6,5},{7,6},{9,8},{10,9},{11,10},{13,12},{... | collective-permute-start | bytes 589832 | tf_op jit(solution)/shard_map/ppermute | solution.py:23
  192.0 21.0 %copy-start.24 = (f32[16,32,384]{2,1,0:T(8,128)S(1)}, f32[16,32,384]{2,1,0:T(8,128)}, u32[]{:S(2)}) copy-start(f32[16,32,384]{2,1,0:T(8,128)} %param.11) | copy-start | bytes 2359300
  192.1 7.9 %collective-permute-start.9 = (f32[4,32,384]{2,1,0:T(8,128)S(1)}, f32[4,32,384]{2,1,0:T(8,128)S(1)}, u32[]{:S(2)}, u32[]{:S(2)}) collective-permute-start(f32[4,32,384]{2,1,0:T(8,128)S(1)} %get-tuple-element.66), channel_id=1, source_target_pairs={{0,1},{1,2},{2,3},{4,5},{5,6},{6,7},{8,9},{9,10},{10,11},{12,13},{... | collective-permute-start | bytes 589832 | tf_op jit(solution)/shard_map/ppermute | solution.py:21
  202.6 6.5 %collective-permute-start.10 = (f32[4,32,384]{2,1,0:T(8,128)S(1)}, f32[4,32,384]{2,1,0:T(8,128)S(1)}, u32[]{:S(2)}, u32[]{:S(2)}) collective-permute-start(f32[4,32,384]{2,1,0:T(8,128)S(1)} %get-tuple-element.60), channel_id=1, source_target_pairs={{0,1},{1,2},{2,3},{4,5},{5,6},{6,7},{8,9},{9,10},{10,11},{12,13},{... | collective-permute-start | bytes 589832 | tf_op jit(solution)/shard_map/ppermute | solution.py:21
  207.8 5.3 collective-permute-start.11
  225.8 8.2 %collective-permute-start.12 = (f32[4,32,384]{2,1,0:T(8,128)S(1)}, f32[4,32,384]{2,1,0:T(8,128)S(1)}, u32[]{:S(2)}, u32[]{:S(2)}) collective-permute-start(f32[4,32,384]{2,1,0:T(8,128)S(1)} %get-tuple-element.58), channel_id=1, source_target_pairs={{1,0},{2,1},{3,2},{5,4},{6,5},{7,6},{9,8},{10,9},{11,10},{13,12},{... | collective-permute-start | bytes 589832 | tf_op jit(solution)/shard_map/ppermute | solution.py:23
  227.1 21.0 %copy-start.25 = (f32[16,32,384]{2,1,0:T(8,128)S(1)}, f32[16,32,384]{2,1,0:T(8,128)}, u32[]{:S(2)}) copy-start(f32[16,32,384]{2,1,0:T(8,128)} %param.11) | copy-start | bytes 2359300
  227.2 7.9 %collective-permute-start.13 = (f32[4,32,384]{2,1,0:T(8,128)S(1)}, f32[4,32,384]{2,1,0:T(8,128)S(1)}, u32[]{:S(2)}, u32[]{:S(2)}) collective-permute-start(f32[4,32,384]{2,1,0:T(8,128)S(1)} %get-tuple-element.59), channel_id=1, source_target_pairs={{0,1},{1,2},{2,3},{4,5},{5,6},{6,7},{8,9},{9,10},{10,11},{12,13},{... | collective-permute-start | bytes 589832 | tf_op jit(solution)/shard_map/ppermute | solution.py:21
  237.7 6.5 %collective-permute-start.14 = (f32[4,32,384]{2,1,0:T(8,128)S(1)}, f32[4,32,384]{2,1,0:T(8,128)S(1)}, u32[]{:S(2)}, u32[]{:S(2)}) collective-permute-start(f32[4,32,384]{2,1,0:T(8,128)S(1)} %get-tuple-element.53), channel_id=1, source_target_pairs={{0,1},{1,2},{2,3},{4,5},{5,6},{6,7},{8,9},{9,10},{10,11},{12,13},{... | collective-permute-start | bytes 589832 | tf_op jit(solution)/shard_map/ppermute | solution.py:21
  242.9 5.3 collective-permute-start.15
  261.0 8.6 %collective-permute-start.16 = (f32[4,32,384]{2,1,0:T(8,128)S(1)}, f32[4,32,384]{2,1,0:T(8,128)S(1)}, u32[]{:S(2)}, u32[]{:S(2)}) collective-permute-start(f32[4,32,384]{2,1,0:T(8,128)S(1)} %get-tuple-element.51), channel_id=1, source_target_pairs={{1,0},{2,1},{3,2},{5,4},{6,5},{7,6},{9,8},{10,9},{11,10},{13,12},{... | collective-permute-start | bytes 589832 | tf_op jit(solution)/shard_map/ppermute | solution.py:23
  262.3 21.1 %copy-start.26 = (f32[16,32,384]{2,1,0:T(8,128)S(1)}, f32[16,32,384]{2,1,0:T(8,128)}, u32[]{:S(2)}) copy-start(f32[16,32,384]{2,1,0:T(8,128)} %param.11) | copy-start | bytes 2359300
  262.3 7.9 %collective-permute-start.17 = (f32[4,32,384]{2,1,0:T(8,128)S(1)}, f32[4,32,384]{2,1,0:T(8,128)S(1)}, u32[]{:S(2)}, u32[]{:S(2)}) collective-permute-start(f32[4,32,384]{2,1,0:T(8,128)S(1)} %get-tuple-element.52), channel_id=1, source_target_pairs={{0,1},{1,2},{2,3},{4,5},{5,6},{6,7},{8,9},{9,10},{10,11},{12,13},{... | collective-permute-start | bytes 589832 | tf_op jit(solution)/shard_map/ppermute | solution.py:21
  272.8 6.5 %collective-permute-start.18 = (f32[4,32,384]{2,1,0:T(8,128)S(1)}, f32[4,32,384]{2,1,0:T(8,128)S(1)}, u32[]{:S(2)}, u32[]{:S(2)}) collective-permute-start(f32[4,32,384]{2,1,0:T(8,128)S(1)} %get-tuple-element.46), channel_id=1, source_target_pairs={{0,1},{1,2},{2,3},{4,5},{5,6},{6,7},{8,9},{9,10},{10,11},{12,13},{... | collective-permute-start | bytes 589832 | tf_op jit(solution)/shard_map/ppermute | solution.py:21
  278.0 5.3 collective-permute-start.19
  299.6 8.2 %collective-permute-start.20 = (f32[4,32,384]{2,1,0:T(8,128)S(1)}, f32[4,32,384]{2,1,0:T(8,128)S(1)}, u32[]{:S(2)}, u32[]{:S(2)}) collective-permute-start(f32[4,32,384]{2,1,0:T(8,128)S(1)} %get-tuple-element.44), channel_id=1, source_target_pairs={{1,0},{2,1},{3,2},{5,4},{6,5},{7,6},{9,8},{10,9},{11,10},{13,12},{... | collective-permute-start | bytes 589832 | tf_op jit(solution)/shard_map/ppermute | solution.py:23
  300.9 21.1 %copy-start.27 = (f32[16,32,384]{2,1,0:T(8,128)S(1)}, f32[16,32,384]{2,1,0:T(8,128)}, u32[]{:S(2)}) copy-start(f32[16,32,384]{2,1,0:T(8,128)} %param.11) | copy-start | bytes 2359300
  300.9 7.9 %collective-permute-start.21 = (f32[4,32,384]{2,1,0:T(8,128)S(1)}, f32[4,32,384]{2,1,0:T(8,128)S(1)}, u32[]{:S(2)}, u32[]{:S(2)}) collective-permute-start(f32[4,32,384]{2,1,0:T(8,128)S(1)} %get-tuple-element.45), channel_id=1, source_target_pairs={{0,1},{1,2},{2,3},{4,5},{5,6},{6,7},{8,9},{9,10},{10,11},{12,13},{... | collective-permute-start | bytes 589832 | tf_op jit(solution)/shard_map/ppermute | solution.py:21
  311.4 6.5 %collective-permute-start.22 = (f32[4,32,384]{2,1,0:T(8,128)S(1)}, f32[4,32,384]{2,1,0:T(8,128)S(1)}, u32[]{:S(2)}, u32[]{:S(2)}) collective-permute-start(f32[4,32,384]{2,1,0:T(8,128)S(1)} %get-tuple-element.39), channel_id=1, source_target_pairs={{0,1},{1,2},{2,3},{4,5},{5,6},{6,7},{8,9},{9,10},{10,11},{12,13},{... | collective-permute-start | bytes 589832 | tf_op jit(solution)/shard_map/ppermute | solution.py:21
  316.6 5.3 collective-permute-start.23
  338.2 8.3 %collective-permute-start.24 = (f32[4,32,384]{2,1,0:T(8,128)S(1)}, f32[4,32,384]{2,1,0:T(8,128)S(1)}, u32[]{:S(2)}, u32[]{:S(2)}) collective-permute-start(f32[4,32,384]{2,1,0:T(8,128)S(1)} %get-tuple-element.37), channel_id=1, source_target_pairs={{1,0},{2,1},{3,2},{5,4},{6,5},{7,6},{9,8},{10,9},{11,10},{13,12},{... | collective-permute-start | bytes 589832 | tf_op jit(solution)/shard_map/ppermute | solution.py:23
  339.5 19.1 %copy-start.48 = (bf16[1,8,16,32,384]{4,3,2,1,0:T(8,128)(2,1)S(1)}, bf16[1,8,16,32,384]{4,3,2,1,0:T(8,128)(2,1)}, u32[]{:S(2)}) copy-start(bf16[1,8,16,32,384]{4,3,2,1,0:T(8,128)(2,1)} %param.17) | copy-start | bytes 9437188
  339.5 8.0 %collective-permute-start.25 = (f32[4,32,384]{2,1,0:T(8,128)S(1)}, f32[4,32,384]{2,1,0:T(8,128)S(1)}, u32[]{:S(2)}, u32[]{:S(2)}) collective-permute-start(f32[4,32,384]{2,1,0:T(8,128)S(1)} %get-tuple-element.38), channel_id=1, source_target_pairs={{0,1},{1,2},{2,3},{4,5},{5,6},{6,7},{8,9},{9,10},{10,11},{12,13},{... | collective-permute-start | bytes 589832 | tf_op jit(solution)/shard_map/ppermute | solution.py:21
  351.9 10.1 %collective-permute-start.26 = (f32[4,32,384]{2,1,0:T(8,128)}, f32[4,32,384]{2,1,0:T(8,128)S(1)}, u32[]{:S(2)}, u32[]{:S(2)}) collective-permute-start(f32[4,32,384]{2,1,0:T(8,128)} %get-tuple-element.32), channel_id=1, source_target_pairs={{0,1},{1,2},{2,3},{4,5},{5,6},{6,7},{8,9},{9,10},{10,11},{12,13},{... | collective-permute-start | bytes 589832 | tf_op jit(solution)/shard_map/ppermute | solution.py:21
  357.1 5.5 collective-permute-start.27
  386.3 9.3 %collective-permute-start.28 = (f32[4,32,384]{2,1,0:T(8,128)S(1)}, f32[4,32,384]{2,1,0:T(8,128)S(1)}, u32[]{:S(2)}, u32[]{:S(2)}) collective-permute-start(f32[4,32,384]{2,1,0:T(8,128)S(1)} %get-tuple-element.30), channel_id=1, source_target_pairs={{1,0},{2,1},{3,2},{5,4},{6,5},{7,6},{9,8},{10,9},{11,10},{13,12},{... | collective-permute-start | bytes 589832 | tf_op jit(solution)/shard_map/ppermute | solution.py:23
  387.6 8.0 %collective-permute-start.29 = (f32[4,32,384]{2,1,0:T(8,128)S(1)}, f32[4,32,384]{2,1,0:T(8,128)S(1)}, u32[]{:S(2)}, u32[]{:S(2)}) collective-permute-start(f32[4,32,384]{2,1,0:T(8,128)S(1)} %get-tuple-element.31), channel_id=1, source_target_pairs={{0,1},{1,2},{2,3},{4,5},{5,6},{6,7},{8,9},{9,10},{10,11},{12,13},{... | collective-permute-start | bytes 589832 | tf_op jit(solution)/shard_map/ppermute | solution.py:21
  400.0 32.3 %collective-permute-start.30 = (f32[4,32,384]{2,1,0:T(8,128)}, f32[4,32,384]{2,1,0:T(8,128)S(1)}, u32[]{:S(2)}, u32[]{:S(2)}) collective-permute-start(f32[4,32,384]{2,1,0:T(8,128)} %get-tuple-element.25), channel_id=1, source_target_pairs={{0,1},{1,2},{2,3},{4,5},{5,6},{6,7},{8,9},{9,10},{10,11},{12,13},{... | collective-permute-start | bytes 589832 | tf_op jit(solution)/shard_map/ppermute | solution.py:21
  405.1 27.2 %collective-permute-start.31 = (f32[4,32,384]{2,1,0:T(8,128)}, f32[4,32,384]{2,1,0:T(8,128)S(1)}, u32[]{:S(2)}, u32[]{:S(2)}) collective-permute-start(f32[4,32,384]{2,1,0:T(8,128)} %get-tuple-element.26), channel_id=1, source_target_pairs={{1,0},{2,1},{3,2},{5,4},{6,5},{7,6},{9,8},{10,9},{11,10},{13,12},{... | collective-permute-start | bytes 589832 | tf_op jit(solution)/shard_map/ppermute | solution.py:23
  461.0 130.6 %reduce-scatter.5.cloned.1.call-start = ((), (), s32[]{:S(2)}) async-start(), calls=%async_computation.5 | async-start | bytes 884736 | tf_op jit(solution)/shard_map/reduce_scatter | solution.py:177
  (42 other events, 369.3 us)
Sparse Core Ops, SparseCore 0:
  461.1 65.4 reduce-scatter.2
  530.3 61.3 reduce-scatter.4
where the time goes:
time: 612 us; the launch traced here: 600 us
  other arithmetic  165 us (27%)
  local copies, waits for them, and re-layouts  150 us (25%)
  waiting for transfers between devices  144 us (24%)
  starting transfers between devices  124 us (20%)
  between operations  15.3 us (2%)
    ppermute x16, starting transfers between devices, padded(): lax.ppermute(tail, axis, [(i, (i + 1) % count) for i in range(ends)])  89.8 us
    reduce_scatter x1, waiting for transfers between devices, local(): lax.psum_scatter(flat_light, 'shot', scatter_dimension=1, tiled=True)  65 us
    scatter x1, local copies, waits for them, and re-layouts, local(): row_buffer = jnp.zeros((device_count, capacity, sample_count), jnp.float3...  56.9 us
    reduce_scatter x1, waiting for transfers between devices, local(): lax.psum_scatter(muted_image, 'shot', scatter_dimension=1, tiled=True)  50 us
    mul x8, other arithmetic, local(): stiffness * divergence  48.6 us
    scatter-add x8, other arithmetic, local(): change = (stiffness * divergence).reshape(-1).at[place_index].add(step_va...  48.2 us
    reshape x31, local copies, waits for them, and re-layouts, local(): change = (stiffness * divergence).reshape(-1).at[place_index].add(step_va...  44.5 us
    mul x8, other arithmetic, local_divergence(): buoyancy * forward_difference(pad_along(wave_field, dimension, 4), dimens...  32.3 us
  transfers between devices with their start and end apart: 36, of which 15 were waited for; matrix products, arithmetic and copies ran while one was open for 26% of the time, Pallas kernels for 0%

commit v1 on v0

v1 whole, which is shorter than its diff:
```python
import functools

import jax
import jax.numpy as jnp
from jax import lax
from jax.experimental import pallas as pl
from jax.experimental.pallas import tpu as pltpu
from jax.sharding import PartitionSpec as P

MUTE = 6
COEFFS = (1225.0 / 1024.0, -245.0 / 3072.0, 49.0 / 5120.0, -5.0 / 7168.0)
RATIOS = tuple(c / COEFFS[0] for c in COEFFS)
SCALE = COEFFS[0] * COEFFS[0]
DAMP = 0.1
LANES = 128
HALO = 7
PAD = 8
MESH = pl.DeviceIdType.MESH


def trace_kernel(sample_count, step_count):
    sample_pos = jnp.arange(sample_count, dtype=jnp.float32)[:, None]
    centers = (jnp.arange(step_count, dtype=jnp.float32)[None, :] + 0.5) * (
        sample_count / step_count
    )
    return 0.25 * jnp.exp(-jnp.abs(sample_pos - centers) / (sample_count / 8.0))


def weighted(pairs):
    total = pairs[0][0] - pairs[0][1]
    for ratio, (ahead, behind) in zip(RATIOS[1:], pairs[1:]):
        total = total + ratio * (ahead - behind)
    return total


def shifted(chunks, amount, lane):
    if amount == 0:
        return chunks
    rolled = [pltpu.roll(chunk, (-amount) % LANES, 1) for chunk in chunks]
    zero = jnp.zeros_like(chunks[0])
    out = []
    for c in range(len(chunks)):
        if amount > 0:
            other = rolled[c + 1] if c + 1 < len(chunks) else zero
            out.append(jnp.where(lane < LANES - amount, rolled[c], other))
        else:
            other = rolled[c - 1] if c > 0 else zero
            out.append(jnp.where(lane >= -amount, rolled[c], other))
    return out


def scatter_body(chunk_count, plane_rows, place_ref, value_ref, dense_ref):
    dense_ref[...] = jnp.zeros_like(dense_ref)
    lane = lax.broadcasted_iota(jnp.int32, (8, LANES), 1)

    def block(group, carry):
        tile = value_ref[group]

        def one(slot, inner):
            cell = place_ref[group * LANES + slot]
            spot = cell // LANES
            at = cell - spot * LANES
            row = (spot % chunk_count) * plane_rows + spot // chunk_count
            moved = pltpu.roll(tile, (at - slot + LANES) % LANES, 1)
            dense_ref[row] = dense_ref[row] + jnp.where(lane == at, moved, 0.0)
            return inner

        return lax.fori_loop(0, LANES, one, carry, unroll=8)

    lax.fori_loop(0, value_ref.shape[0], block, 0)


def wave_body(
    dims,
    stiff_hbm, first_hbm, second_hbm, third_hbm, before_hbm, current_hbm, forward_hbm,
    inject_hbm, source_ref,
    image_out, light_out, earlier_out, latest_out,
    field, stiff, first, second, third, partial, image, light, forward, inject, flux,
    load_sem, store_sem, edge_send, edge_recv, face_send, face_recv,
):
    steps, depth, rows, chunk_count = dims
    sub = lax.axis_index("sub")
    ends = lax.axis_size("sub") - 1
    has_left = sub > 0
    has_right = sub < ends
    zero_tile = jnp.zeros((8, LANES), jnp.float32)

    for c in range(chunk_count):
        def clear(plane, carry, c=c):
            for b in range(2):
                field[b, c, plane, 0:PAD, :] = zero_tile
                field[b, c, plane, PAD + rows:2 * PAD + rows, :] = zero_tile
            return carry
        lax.fori_loop(HALO, HALO + depth, clear, 0)
        for plane in list(range(HALO)) + list(range(HALO + depth, 2 * HALO + depth)):
            for b in range(2):
                field[b, c, plane] = jnp.zeros((2 * PAD + rows, LANES), jnp.float32)
        for face in list(range(4)) + list(range(4 + depth, 7 + depth)):
            first[c, face] = jnp.zeros((rows, LANES), jnp.float32)
        flux[c] = jnp.zeros((2 * PAD + rows, LANES), jnp.float32)

    barrier = pltpu.get_barrier_semaphore()

    @pl.when(has_left)
    def _():
        pl.semaphore_signal(barrier, inc=1, device_id={"sub": sub - 1}, device_id_type=MESH)

    @pl.when(has_right)
    def _():
        pl.semaphore_signal(barrier, inc=1, device_id={"sub": sub + 1}, device_id_type=MESH)

    def lanes(c):
        return pl.ds(c * LANES, LANES)

    inner = pl.ds(PAD, rows)
    loads = []

    def load(src, dst):
        copy = pltpu.make_async_copy(src, dst, load_sem.at[len(loads)])
        copy.start()
        loads.append(copy)

    for c in range(chunk_count):
        load(current_hbm.at[:, :, lanes(c)], field.at[0, c, pl.ds(HALO, depth), inner, :])
        load(third_hbm.at[:, :, lanes(c)], third.at[c])
        load(second_hbm.at[:, :, lanes(c)], second.at[c])
    early = len(loads)
    load(forward_hbm, forward)
    for c in range(chunk_count):
        load(first_hbm.at[:, :, lanes(c)], first.at[c, pl.ds(4, depth)])
        load(stiff_hbm.at[:, :, lanes(c)], stiff.at[c])
        load(before_hbm.at[:, :, lanes(c)], field.at[1, c, pl.ds(HALO, depth), inner, :])
    load(inject_hbm, inject)

    pl.semaphore_wait(barrier, jnp.where(has_left, 1, 0) + jnp.where(has_right, 1, 0))

    def face_copy(side, c):
        if side == 0:
            src = first_hbm.at[pl.ds(0, 3), :, lanes(c)]
            dst = first.at[c, pl.ds(4 + depth, 3)]
            to = sub - 1
        else:
            src = first_hbm.at[pl.ds(depth - 4, 4), :, lanes(c)]
            dst = first.at[c, pl.ds(0, 4)]
            to = sub + 1
        return pltpu.make_async_remote_copy(
            src, dst, face_send.at[side, c], face_recv.at[side, c],
            device_id={"sub": to}, device_id_type=MESH)

    def edge_copy(side, c, b, from_hbm=False):
        start = 0 if side == 0 else depth - HALO
        if from_hbm:
            src = current_hbm.at[pl.ds(start, HALO), :, lanes(c)]
        else:
            src = field.at[b, c, pl.ds(HALO + start, HALO), inner, :]
        dst = field.at[b, c, pl.ds(HALO + depth if side == 0 else 0, HALO), inner, :]
        return pltpu.make_async_remote_copy(
            src, dst, edge_send.at[side, c, b], edge_recv.at[side, c, b],
            device_id={"sub": sub - 1 if side == 0 else sub + 1}, device_id_type=MESH)

    sends_on = (has_left, has_right)
    gets_on = (has_right, has_left)
    for c in range(chunk_count):
        for side in range(2):
            @pl.when(sends_on[side])
            def _(side=side, c=c):
                edge_copy(side, c, 0, True).start()
                face_copy(side, c).start()

    lane = lax.broadcasted_iota(jnp.int32, (8, LANES), 1)
    for copy in loads[:early]:
        copy.wait()

    def inner_part(b, x, carry):
        for y in range(0, rows, 8):
            at = pl.ds(y, 8)
            p = [field[b, c, HALO + x, pl.ds(PAD + y, 8), :] for c in range(chunk_count)]
            pairs = [(shifted(p, k, lane), shifted(p, 1 - k, lane)) for k in range(1, 5)]
            q = [
                third[c, x, at, :] * weighted([(a[c], z[c]) for a, z in pairs])
                for c in range(chunk_count)
            ]
            pairs = [(shifted(q, k - 1, lane), shifted(q, -k, lane)) for k in range(1, 5)]
            for c in range(chunk_count):
                partial[c, x, at, :] = weighted([(a[c], z[c]) for a, z in pairs])
        for c in range(chunk_count):
            for y in range(0, rows, 8):
                def near(s, c=c, y=y):
                    return field[b, c, HALO + x, pl.ds(PAD + y + s, 8), :]
                flux[c, pl.ds(PAD + y, 8), :] = second[c, x, pl.ds(y, 8), :] * weighted(
                    [(near(k), near(1 - k)) for k in range(1, 5)])
        for c in range(chunk_count):
            for y in range(0, rows, 8):
                def near(s, c=c, y=y):
                    return flux[c, pl.ds(PAD + y + s, 8), :]
                at = pl.ds(y, 8)
                partial[c, x, at, :] = partial[c, x, at, :] + weighted(
                    [(near(k - 1), near(-k)) for k in range(1, 5)])
        return carry

    def inner_all(b):
        lax.fori_loop(0, depth, functools.partial(inner_part, b), 0)

    inner_all(0)
    for copy in loads[early:]:
        copy.wait()

    def prepare(x, carry):
        for c in range(chunk_count):
            stiff[c, x] = stiff[c, x] * SCALE
            total = jnp.zeros((rows, LANES), jnp.float32)
            for t in range(steps):
                frame = forward[t, x, :, c * LANES:(c + 1) * LANES].astype(jnp.float32)
                total = total + frame * frame
            light[c, x] = total
            image[c, x] = jnp.zeros((rows, LANES), jnp.float32)
        return carry

    lax.fori_loop(0, depth, prepare, 0)

    for c in range(chunk_count):
        for side in range(2):
            @pl.when(gets_on[side])
            def _(side=side, c=c):
                face_copy(side, c).wait_recv()

            @pl.when(sends_on[side])
            def _(side=side, c=c):
                face_copy(side, c).wait_send()

    def outer_part(c, t, b, half, carry):
        y = pl.multiple_of(half * 16, 16)
        at = pl.ds(y, 16)
        wide = pl.ds(pl.multiple_of(PAD + y, 8), 16)
        p = [field[b, c, i, wide, :] for i in range(8)]
        q = []
        for f in range(-4, depth + 3):
            q.append(first[c, f + 4, at, :] * weighted([(p[3 + k], p[4 - k]) for k in range(1, 5)]))
            x = f - 3
            if x >= 0:
                div = weighted([(q[3 + k], q[4 - k]) for k in range(1, 5)]) + partial[c, x, at, :]
                change = stiff[c, x, at, :] * div + inject[c, x, pl.ds(t + 8 * y, 16, stride=8), :]
                now = p[0]
                past = field[1 - b, c, HALO + x, wide, :]
                field[1 - b, c, HALO + x, wide, :] = (now + now) - past + change
                frame = forward[t, x, at, c * LANES:(c + 1) * LANES].astype(jnp.float32)
                image[c, x, at, :] = image[c, x, at, :] + frame * change
                q = q[1:]
            if f + 1 < depth + 3:
                p = p[1:] + [field[b, c, f + 5 + HALO, wide, :]]
        return carry

    def one_step(t, carry):
        b = lax.rem(t, 2)

        @pl.when(t > 0)
        def _():
            inner_all(b)

        for c in range(chunk_count):
            for side in range(2):
                @pl.when(gets_on[side])
                def _(side=side, c=c):
                    edge_copy(side, c, b).wait_recv()

                @pl.when(sends_on[side])
                def _(side=side, c=c):
                    edge_copy(side, c, b).wait_send()

            lax.fori_loop(0, rows // 16, functools.partial(outer_part, c, t, b), 0)
            for side in range(2):
                @pl.when(jnp.logical_and(sends_on[side], t < steps - 1))
                def _(side=side, c=c):
                    edge_copy(side, c, 1 - b).start()
        return carry

    lax.fori_loop(0, steps, one_step, 0)

    stores = []

    def store(src, dst):
        copy = pltpu.make_async_copy(src, dst, store_sem.at[len(stores)])
        copy.start()
        stores.append(copy)

    for c in range(chunk_count):
        body = pl.ds(HALO, depth)
        store(field.at[(steps - 1) % 2, c, body, inner, :], earlier_out.at[:, :, lanes(c)])
        store(field.at[steps % 2, c, body, inner, :], latest_out.at[:, :, lanes(c)])
        store(light.at[c], light_out.at[:, :, lanes(c)])

    source = [source_ref[i].astype(jnp.float32) for i in range(3)]
    second_at = lax.broadcasted_iota(jnp.int32, (rows, LANES), 0).astype(jnp.float32) - source[1]
    third_at = lax.broadcasted_iota(jnp.int32, (rows, LANES), 1).astype(jnp.float32) - source[2]

    def mute(x, carry):
        first_at = (sub * depth + x).astype(jnp.float32) - source[0]
        base = first_at * first_at + second_at * second_at
        for c in range(chunk_count):
            along = third_at + float(c * LANES)
            distance = base + along * along
            image[c, x] = image[c, x] * (1.0 - jnp.exp(-distance / (2.0 * MUTE * MUTE)))
        return carry

    lax.fori_loop(0, depth, mute, 0)
    for c in range(chunk_count):
        store(image.at[c], image_out.at[:, :, lanes(c)])
    for copy in stores:
        copy.wait()


def local(
    stiffness, buoyancy_first, buoyancy_second, buoyancy_third, adjoint_before,
    adjoint_current, forward_field, traces, receiver_target, receiver_cell, source_cell,
):
    device_count = lax.axis_size(("shot", "sub"))
    sample_count = traces.shape[1]
    steps = forward_field.shape[1]
    depth, rows, length = stiffness.shape
    chunk_count = length // LANES
    row_count = traces.shape[0]
    capacity = max(2, (3 * row_count + 2 * device_count - 1) // (2 * device_count))
    slots = device_count * capacity

    kernel = trace_kernel(sample_count, steps)
    values = jnp.dot(
        traces, kernel, precision=lax.Precision.HIGHEST, preferred_element_type=jnp.float32)
    target = receiver_target[:, 0]
    onehot = target[:, None] == jnp.arange(device_count, dtype=jnp.int32)[None, :]
    row_ids = jnp.arange(row_count, dtype=jnp.int32)
    lower = (row_ids[:, None] >= row_ids[None, :]).astype(jnp.bfloat16)
    running = jnp.dot(lower, onehot.astype(jnp.bfloat16), preferred_element_type=jnp.float32)
    slot = (jnp.sum(jnp.where(onehot, running, 0.0), axis=1) - 1.0).astype(jnp.int32)
    chosen = (
        (target * capacity + slot)[None, :] == jnp.arange(slots, dtype=jnp.int32)[:, None]
    ).astype(jnp.float32)
    rows_out = jnp.concatenate([values, receiver_cell.astype(jnp.float32)[:, None]], axis=1)
    packed = jnp.dot(
        chosen, rows_out, precision=lax.Precision.HIGHEST, preferred_element_type=jnp.float32)
    got = lax.all_to_all(
        packed.reshape(device_count, capacity * (steps + 1)), ("shot", "sub"),
        split_axis=0, concat_axis=0, tiled=True).reshape(slots, steps + 1)
    groups = -(-slots // LANES)
    got = jnp.pad(got, ((0, groups * LANES - slots), (0, 0)))
    places = (got[:, steps] + 0.5).astype(jnp.int32)
    tiles = got[:, :steps].T.reshape(steps, groups, LANES).transpose(1, 0, 2)

    dense = pl.pallas_call(
        functools.partial(scatter_body, chunk_count, depth * rows),
        out_shape=jax.ShapeDtypeStruct((chunk_count * depth * rows, steps, LANES), jnp.float32),
        in_specs=[pl.BlockSpec(memory_space=pltpu.SMEM), pl.BlockSpec(memory_space=pltpu.VMEM)],
        out_specs=pl.BlockSpec(memory_space=pltpu.VMEM),
        compiler_params=pltpu.CompilerParams(vmem_limit_bytes=32 * 2**20),
    )(places, tiles).reshape(chunk_count, depth, rows * steps, LANES)

    f32 = jnp.float32
    grid_shape = jax.ShapeDtypeStruct((depth, rows, length), f32)
    anywhere = pl.BlockSpec(memory_space=pl.ANY)
    cells = (chunk_count, depth, rows, LANES)
    image, light, earlier, latest = pl.pallas_call(
        functools.partial(wave_body, (steps, depth, rows, chunk_count)),
        out_shape=[grid_shape] * 4,
        in_specs=[anywhere] * 8 + [pl.BlockSpec(memory_space=pltpu.SMEM)],
        out_specs=[anywhere] * 4,
        scratch_shapes=[
            pltpu.VMEM((2, chunk_count, depth + 2 * HALO, rows + 2 * PAD, LANES), f32),
            pltpu.VMEM(cells, f32),
            pltpu.VMEM((chunk_count, depth + 7, rows, LANES), f32),
            pltpu.VMEM(cells, f32),
            pltpu.VMEM(cells, f32),
            pltpu.VMEM(cells, f32),
            pltpu.VMEM(cells, f32),
            pltpu.VMEM(cells, f32),
            pltpu.VMEM((steps, depth, rows, length), jnp.bfloat16),
            pltpu.VMEM((chunk_count, depth, rows * steps, LANES), f32),
            pltpu.VMEM((chunk_count, rows + 2 * PAD, LANES), f32),
            pltpu.SemaphoreType.DMA((6 * chunk_count + 2,)),
            pltpu.SemaphoreType.DMA((4 * chunk_count,)),
            pltpu.SemaphoreType.DMA((2, chunk_count, 2)),
            pltpu.SemaphoreType.DMA((2, chunk_count, 2)),
            pltpu.SemaphoreType.DMA((2, chunk_count)),
            pltpu.SemaphoreType.DMA((2, chunk_count)),
        ],
        compiler_params=pltpu.CompilerParams(
            collective_id=0, has_side_effects=True, vmem_limit_bytes=48 * 2**20),
    )(
        stiffness, buoyancy_first, buoyancy_second, buoyancy_third, adjoint_before[0],
        adjoint_current[0], forward_field[0], dense, source_cell[0],
    )
    summed_image = lax.psum_scatter(image.reshape(depth, -1), "shot", scatter_dimension=1, tiled=True)
    summed_light = lax.psum_scatter(light.reshape(depth, -1), "shot", scatter_dimension=1, tiled=True)
    gradient = summed_image / (summed_light / (steps * lax.axis_size("shot")) + DAMP)
    return (gradient, earlier[None], latest[None])


def solution(mesh):
    placed = (
        P("sub", None, None),
        P("sub", None, None),
        P("sub", None, None),
        P("sub", None, None),
        P("shot", "sub", None, None),
        P("shot", "sub", None, None),
        P("shot", None, "sub", None, None),
        P(("shot", "sub"), None),
        P(("shot", "sub"), None),
        P(("shot", "sub")),
        P("shot", None),
    )
    return jax.shard_map(
        local,
        mesh=mesh,
        in_specs=placed,
        out_specs=(P("sub", "shot"), P("shot", "sub", None, None), P("shot", "sub", None, None)),
        check_vma=False,
    )
```

time: 612 us -> 245 us (0.40); the launches traced: 600 us -> 245 us
  other arithmetic: 165 us -> 3.36 us
  local copies, waits for them, and re-layouts: 150 us -> 7.69 us
  starting transfers between devices: 124 us -> 0.08 us
  Pallas kernels: 0 us -> 78.3 us
  waiting for transfers between devices: 144 us -> 125 us
  blocking collectives: 0 us -> 14.4 us
    ppermute x32 -> x0, starting transfers between devices: 111 us -> none  [the longest x16 89.8 us: padded(): lax.ppermute(tail, axis, [(i, (i + 1) % count) for i in range(ends)])]
    scatter x2 -> x0, local copies, waits for them, and re-layouts: 82 us -> none  [the longest x1 56.9 us: local(): row_buffer = jnp.zeros((device_count, capacity, sample_count), jnp.float3...]
    mul x16 -> x0, other arithmetic: 80.9 us -> none  [the longest x8 48.6 us: local(): stiffness * divergence]
    pallas_call x0 -> x2, Pallas kernels: none -> 78.3 us  [the longest x1 63.9 us: local(): pl.pallas_call(functools.partial(wave_body, (steps, depth, rows, chunk_co...]
    scatter-add x8 -> x0, other arithmetic: 48.2 us -> none  [local(): change = (stiffness * divergence).reshape(-1).at[place_index].add(step_va...]
    reshape x31 -> x1, local copies, waits for them, and re-layouts: 44.5 us -> 0.17 us  [local(): got = lax.all_to_all(packed.reshape(device_count, capacity * (steps + 1))...]
    ppermute x32 -> x0, waiting for transfers between devices: 28.4 us -> none  [the longest x16 22.6 us: padded(): lax.ppermute(head, axis, [((i + 1) % count, i) for i in range(ends)])]
    add x11 -> x1, other arithmetic: 27.3 us -> 0.69 us  [local(): target * capacity + slot]
  transfers between devices with their start and end apart: 36 -> 2, of which waited for: 15 -> 2; matrix products, arithmetic and copies ran while one was open for 26% -> 1% of each run, Pallas kernels for 0% -> 0%
where the time goes in v1:
time: 245 us
  waiting for transfers between devices  125 us (51%)
  Pallas kernels  78.3 us (32%)
  blocking collectives  14.4 us (6%)
  between operations  14.1 us (6%)
  local copies, waits for them, and re-layouts  7.69 us (3%)
  other arithmetic  3.36 us (1%)
    reduce_scatter x1, waiting for transfers between devices, local(): lax.psum_scatter(image.reshape(depth, -1), 'shot', scatter_dimension=1, t...  65.8 us
    pallas_call x1, Pallas kernels, local(): pl.pallas_call(functools.partial(wave_body, (steps, depth, rows, chunk_co...  63.9 us
    reduce_scatter x1, waiting for transfers between devices, local(): lax.psum_scatter(light.reshape(depth, -1), 'shot', scatter_dimension=1, t...  58.7 us
    all_to_all x1, blocking collectives, local(): lax.all_to_all(packed.reshape(device_count, capacity * (steps + 1)), ('sh...  14.4 us
    pallas_call x1, Pallas kernels, local(): pl.pallas_call(functools.partial(scatter_body, chunk_count, depth * rows)...  14.3 us
    unnamed x16, local copies, waits for them, and re-layouts  7.12 us
  transfers between devices with their start and end apart: 2, of which 2 were waited for; matrix products, arithmetic and copies ran while one was open for 1% of the time, Pallas kernels for 0%

profile of v1, /device:TPU:0, one launch (start us, length us, event | category | flops | bytes accessed | tf_op | source)
XLA Modules:
  0.0 244.8 jit_solution(17059015154253790522)
XLA Ops:
  7.2 0.0 copy-start
  7.2 0.0 reduce-scatter.5.cloned.1.call-start
  7.2 1.0 fusion.1
  8.3 0.7 convert_add_fusion
  9.0 0.7 convert_element_type.19
  9.6 0.0 copy-done
  9.6 0.5 convolution_bitcast_fusion
  10.2 0.8 fusion
  11.0 0.2 all_to_all.8
  11.2 14.4 %all_to_all.10 = f32[32,1,216]{2,1,0:T(1,128)S(1)} all-to-all(f32[32,1,216]{2,1,0:T(1,128)S(1)} %all_to_all.8), channel_id=1, replica_groups=mesh['shot'=8,'sub'=4] {'shot','sub'}, dimensions={0} | all-to-all | bytes 55296 | tf_op jit(solution)/shard_map/all_to_all | solution.py:340
  25.6 0.1 reduce
  25.7 0.2 reshape.46
  25.8 0.3 fusion.4.place_ref
  26.2 0.1 copy.21
  26.3 0.0 copy-start.2
  26.3 0.0 copy-start.3
  26.3 0.0 copy-start.4
  26.3 0.0 copy-start.5
  26.3 14.3 %shard_map.130 = f32[1536,8,128]{2,1,0:T(8,128)S(1)} custom-call(s32[768]{0:T(1024)S(1)} %fusion.4.place_ref, f32[6,8,128]{2,1,0:T(8,128)S(1)} %bitcast.26), custom_call_target="tpu_custom_call" | custom-call | tf_op jit(solution)/shard_map/pallas_call | solution.py:348
  40.7 0.0 copy-start.1
  40.7 2.7 %copy-done.1 = f32[1536,8,128]{2,1,0:T(8,128)} copy-done((f32[1536,8,128]{2,1,0:T(8,128)}, f32[1536,8,128]{2,1,0:T(8,128)S(1)}, u32[]{:S(2)}) %copy-start.1) | copy-done | bytes 6291480
  43.3 0.0 copy-done.2
  43.3 0.0 copy-done.3
  43.3 0.0 copy-done.4
  43.3 0.0 copy-done.5
  43.3 63.9 %shard_map.131 = (f32[16,32,384]{2,1,0:T(8,128)S(1)}, f32[16,32,384]{2,1,0:T(8,128)S(1)}, f32[16,32,384]{2,1,0:T(8,128)S(1)}, f32[16,32,384]{2,1,0:T(8,128)S(1)}) custom-call(f32[16,32,384]{2,1,0:T(8,128)S(1)} %copy-done.2, f32[16,32,384]{2,1,0:T(8,128)S(1)} %copy-done.3, f32[16,32,384]{2,1,0:T(8,128)S(1)} %copy-done.4, f32[16,32,384]{2,1,0:T(8,128)} %third_hbm.1, ...), custom_call_target="tpu_custom_call" | custom-call | tf_op jit(solution)/shard_map/pallas_call | solution.py:360
  107.3 1.3 copy.24
  108.6 0.0 reduce-scatter.5.cloned.1.call-update
  108.6 0.0 reduce-scatter.3.cloned.1.call-start
  108.7 1.3 copy.23
  110.0 0.0 reduce-scatter.3.cloned.1.call-update
  110.0 58.7 %reduce-scatter.5.cloned.1.call-done = f32[16,1536]{1,0:T(8,128)} async-done(((f32[16,12288]{1,0:T(8,128)}), f32[16,1536]{1,0:T(8,128)}) %reduce-scatter.5.cloned.1.call-update) | async-done | bytes 98320 | tf_op jit(solution)/shard_map/reduce_scatter | solution.py:391
  168.8 65.8 %reduce-scatter.3.cloned.1.call-done = f32[16,1536]{1,0:T(8,128)} async-done(((f32[16,12288]{1,0:T(8,128)}), f32[16,1536]{1,0:T(8,128)}) %reduce-scatter.3.cloned.1.call-update) | async-done | bytes 98320 | tf_op jit(solution)/shard_map/reduce_scatter | solution.py:390
  234.6 1.6 add_divide_fusion
  236.2 0.9 copy.27
  237.1 0.9 copy.28
  (2 shorter events, 0.0 us)
Async XLA Ops:
  7.2 2.5 %copy-start = (f32[512,256]{1,0:T(8,128)S(1)}, f32[512,256]{1,0:T(8,128)}, u32[]{:S(2)}) copy-start(f32[512,256]{1,0:T(8,128)} %param.18) | copy-start | bytes 1572868
  7.2 161.6 %reduce-scatter.5.cloned.1.call-start = ((), (), s32[]{:S(2)}) async-start(), calls=%async_computation.4 | async-start | bytes 884736 | tf_op jit(solution)/shard_map/reduce_scatter | solution.py:391
  26.3 17.0 %copy-start.2 = (f32[16,32,384]{2,1,0:T(8,128)S(1)}, f32[16,32,384]{2,1,0:T(8,128)}, u32[]{:S(2)}) copy-start(f32[16,32,384]{2,1,0:T(8,128)} %stiff_hbm.1) | copy-start | bytes 2359300
  26.3 17.0 %copy-start.3 = (f32[16,32,384]{2,1,0:T(8,128)S(1)}, f32[16,32,384]{2,1,0:T(8,128)}, u32[]{:S(2)}) copy-start(f32[16,32,384]{2,1,0:T(8,128)} %first_hbm.1) | copy-start | bytes 2359300
  26.3 17.0 %copy-start.4 = (f32[16,32,384]{2,1,0:T(8,128)S(1)}, f32[16,32,384]{2,1,0:T(8,128)}, u32[]{:S(2)}) copy-start(f32[16,32,384]{2,1,0:T(8,128)} %second_hbm.1) | copy-start | bytes 2359300
  26.3 17.0 %copy-start.5 = (s32[1,3]{1,0:T(1,128)S(1)}, s32[1,3]{1,0:T(1,128)}, u32[]{:S(2)}) copy-start(s32[1,3]{1,0:T(1,128)} %param.21) | copy-start | bytes 40
  40.7 2.7 %copy-start.1 = (f32[1536,8,128]{2,1,0:T(8,128)}, f32[1536,8,128]{2,1,0:T(8,128)S(1)}, u32[]{:S(2)}) copy-start(f32[1536,8,128]{2,1,0:T(8,128)S(1)} %shard_map.130) | copy-start | bytes 18874372
  108.6 126.0 %reduce-scatter.3.cloned.1.call-start = ((), (), s32[]{:S(2)}) async-start(), calls=%async_computation.3 | async-start | bytes 884736 | tf_op jit(solution)/shard_map/reduce_scatter | solution.py:390
Sparse Core Ops, SparseCore 0:
  108.7 59.9 reduce-scatter.4
  173.0 61.5 reduce-scatter.2

commit v2 on v1

--- a/solution.py
+++ b/solution.py
@@ -49,7 +49,7 @@
     return out
 
 
-def scatter_body(chunk_count, plane_rows, place_ref, value_ref, dense_ref):
+def scatter_body(row_ref, at_ref, turn_ref, value_ref, dense_ref):
     dense_ref[...] = jnp.zeros_like(dense_ref)
     lane = lax.broadcasted_iota(jnp.int32, (8, LANES), 1)
 
@@ -57,12 +57,10 @@
         tile = value_ref[group]
 
         def one(slot, inner):
-            cell = place_ref[group * LANES + slot]
-            spot = cell // LANES
-            at = cell - spot * LANES
-            row = (spot % chunk_count) * plane_rows + spot // chunk_count
-            moved = pltpu.roll(tile, (at - slot + LANES) % LANES, 1)
-            dense_ref[row] = dense_ref[row] + jnp.where(lane == at, moved, 0.0)
+            number = group * LANES + slot
+            row = row_ref[number]
+            moved = pltpu.roll(tile, turn_ref[number], 1)
+            dense_ref[row] = dense_ref[row] + jnp.where(lane == at_ref[number], moved, 0.0)
             return inner
 
         return lax.fori_loop(0, LANES, one, carry, unroll=8)
@@ -74,11 +72,17 @@
     dims,
     stiff_hbm, first_hbm, second_hbm, third_hbm, before_hbm, current_hbm, forward_hbm,
     inject_hbm, source_ref,
-    image_out, light_out, earlier_out, latest_out,
-    field, stiff, first, second, third, partial, image, light, forward, inject, flux,
+    gradient_out, earlier_out, latest_out,
+    field, stiff, first, second, third, partial, image, forward, inject, flux,
+    light_blocks, light_got, image_blocks, image_got, image_last,
     load_sem, store_sem, edge_send, edge_recv, face_send, face_recv,
+    light_send, light_recv, across_send, across_recv, along_send, along_recv,
 ):
-    steps, depth, rows, chunk_count = dims
+    steps, depth, rows, chunk_count, lines, columns = dims
+    shots = lines * columns
+    share = rows // shots
+    shot = lax.axis_index("shot")
+    line, column = lax.div(shot, columns), lax.rem(shot, columns)
     sub = lax.axis_index("sub")
     ends = lax.axis_size("sub") - 1
     has_left = sub > 0
@@ -109,6 +113,10 @@
     def _():
         pl.semaphore_signal(barrier, inc=1, device_id={"sub": sub + 1}, device_id_type=MESH)
 
+    for k in range(1, shots):
+        pl.semaphore_signal(
+            barrier, inc=1, device_id={"shot": lax.rem(shot + k, shots)}, device_id_type=MESH)
+
     def lanes(c):
         return pl.ds(c * LANES, LANES)
 
@@ -132,7 +140,8 @@
         load(before_hbm.at[:, :, lanes(c)], field.at[1, c, pl.ds(HALO, depth), inner, :])
     load(inject_hbm, inject)
 
-    pl.semaphore_wait(barrier, jnp.where(has_left, 1, 0) + jnp.where(has_right, 1, 0))
+    pl.semaphore_wait(
+        barrier, (shots - 1) + jnp.where(has_left, 1, 0) + jnp.where(has_right, 1, 0))
 
     def face_copy(side, c):
         if side == 0:
@@ -168,6 +177,7 @@
                 face_copy(side, c).start()
 
     lane = lax.broadcasted_iota(jnp.int32, (8, LANES), 1)
+    base = PAD + lax.div(sub, lax.axis_size("sub"))
     for copy in loads[:early]:
         copy.wait()
 
@@ -186,13 +196,13 @@
         for c in range(chunk_count):
             for y in range(0, rows, 8):
                 def near(s, c=c, y=y):
-                    return field[b, c, HALO + x, pl.ds(PAD + y + s, 8), :]
+                    return field[b, c, HALO + x, pl.ds(base + (y + s), 8), :]
                 flux[c, pl.ds(PAD + y, 8), :] = second[c, x, pl.ds(y, 8), :] * weighted(
                     [(near(k), near(1 - k)) for k in range(1, 5)])
         for c in range(chunk_count):
             for y in range(0, rows, 8):
                 def near(s, c=c, y=y):
-                    return flux[c, pl.ds(PAD + y + s, 8), :]
+                    return flux[c, pl.ds(base + (y + s), 8), :]
                 at = pl.ds(y, 8)
                 partial[c, x, at, :] = partial[c, x, at, :] + weighted(
                     [(near(k - 1), near(-k)) for k in range(1, 5)])
@@ -204,6 +214,11 @@
     inner_all(0)
     for copy in loads[early:]:
         copy.wait()
+
+    def put_blocks(blocks, c, x, value):
+        for d in range(shots):
+            blocks[d % columns, c, d // columns, pl.ds(x * share, share), :] = (
+                value[d * share:(d + 1) * share, :])
 
     def prepare(x, carry):
         for c in range(chunk_count):
@@ -212,11 +227,47 @@
             for t in range(steps):
                 frame = forward[t, x, :, c * LANES:(c + 1) * LANES].astype(jnp.float32)
                 total = total + frame * frame
-            light[c, x] = total
+            put_blocks(light_blocks, c, x, total)
             image[c, x] = jnp.zeros((rows, LANES), jnp.float32)
         return carry
 
     lax.fori_loop(0, depth, prepare, 0)
+
+    def light_copy(k):
+        to = lax.rem(shot + k, shots)
+        return pltpu.make_async_remote_copy(
+            light_blocks.at[lax.rem(to, columns), :, lax.div(to, columns)],
+            light_got.at[k - 1], light_send.at[k - 1], light_recv.at[k - 1],
+            device_id={"shot": to}, device_id_type=MESH)
+
+    for k in range(1, shots):
+        light_copy(k).start()
+
+    def across_copy(k, c):
+        to = lax.rem(column + k, columns)
+        return pltpu.make_async_remote_copy(
+            image_blocks.at[to, c], image_got.at[k - 1, c],
+            across_send.at[k - 1, c], across_recv.at[k - 1, c],
+            device_id={"shot": line * columns + to}, device_id_type=MESH)
+
+    def along_copy(k, c):
+        to = lax.rem(line + k, lines)
+        return pltpu.make_async_remote_copy(
+            image_blocks.at[column, c, to], image_last.at[k - 1, c],
+            along_send.at[k - 1, c], along_recv.at[k - 1, c],
+            device_id={"shot": to * columns + column}, device_id_type=MESH)
+
+    source = [source_ref[i].astype(jnp.float32) for i in range(3)]
+    second_at = lax.broadcasted_iota(jnp.int32, (rows, LANES), 0).astype(jnp.float32) - source[1]
+    third_at = lax.broadcasted_iota(jnp.int32, (rows, LANES), 1).astype(jnp.float32) - source[2]
+
+    def mute(c, x, carry):
+        first_at = (sub * depth + x).astype(jnp.float32) - source[0]
+        along = third_at + float(c * LANES)
+        distance = first_at * first_at + second_at * second_at + along * along
+        put_blocks(
+            image_blocks, c, x, image[c, x] * (1.0 - jnp.exp(-distance / (2.0 * MUTE * MUTE))))
+        return carry
 
     for c in range(chunk_count):
         for side in range(2):
@@ -272,6 +323,12 @@
                 @pl.when(jnp.logical_and(sends_on[side], t < steps - 1))
                 def _(side=side, c=c):
                     edge_copy(side, c, 1 - b).start()
+
+            @pl.when(t == steps - 1)
+            def _(c=c):
+                lax.fori_loop(0, depth, functools.partial(mute, c), 0)
+                for k in range(1, columns):
+                    across_copy(k, c).start()
         return carry
 
     lax.fori_loop(0, steps, one_step, 0)
@@ -287,24 +344,24 @@
         body = pl.ds(HALO, depth)
         store(field.at[(steps - 1) % 2, c, body, inner, :], earlier_out.at[:, :, lanes(c)])
         store(field.at[steps % 2, c, body, inner, :], latest_out.at[:, :, lanes(c)])
-        store(light.at[c], light_out.at[:, :, lanes(c)])
-
-    source = [source_ref[i].astype(jnp.float32) for i in range(3)]
-    second_at = lax.broadcasted_iota(jnp.int32, (rows, LANES), 0).astype(jnp.float32) - source[1]
-    third_at = lax.broadcasted_iota(jnp.int32, (rows, LANES), 1).astype(jnp.float32) - source[2]
-
-    def mute(x, carry):
-        first_at = (sub * depth + x).astype(jnp.float32) - source[0]
-        base = first_at * first_at + second_at * second_at
-        for c in range(chunk_count):
-            along = third_at + float(c * LANES)
-            distance = base + along * along
-            image[c, x] = image[c, x] * (1.0 - jnp.exp(-distance / (2.0 * MUTE * MUTE)))
-        return carry
-
-    lax.fori_loop(0, depth, mute, 0)
-    for c in range(chunk_count):
-        store(image.at[c], image_out.at[:, :, lanes(c)])
+
+    for c in range(chunk_count):
+        for k in range(1, columns):
+            across_copy(k, c).wait()
+            image_blocks[column, c] = image_blocks[column, c] + image_got[k - 1, c]
+        for k in range(1, lines):
+            along_copy(k, c).start()
+    for k in range(1, shots):
+        light_copy(k).wait()
+    for c in range(chunk_count):
+        light = light_blocks[column, c, line]
+        for k in range(1, shots):
+            light = light + light_got[k - 1, c]
+        summed = image_blocks[column, c, line]
+        for k in range(1, lines):
+            along_copy(k, c).wait()
+            summed = summed + image_last[k - 1, c]
+        gradient_out[c] = summed / (light / (steps * shots) + DAMP)
     for copy in stores:
         copy.wait()
 
@@ -343,25 +400,36 @@
     groups = -(-slots // LANES)
     got = jnp.pad(got, ((0, groups * LANES - slots), (0, 0)))
     places = (got[:, steps] + 0.5).astype(jnp.int32)
+    spots = places // LANES
+    spot_rows = (spots % chunk_count) * (depth * rows) + spots // chunk_count
+    lane_at = places % LANES
+    turns = (lane_at - jnp.arange(groups * LANES, dtype=jnp.int32)) % LANES
     tiles = got[:, :steps].T.reshape(steps, groups, LANES).transpose(1, 0, 2)
 
     dense = pl.pallas_call(
-        functools.partial(scatter_body, chunk_count, depth * rows),
+        scatter_body,
         out_shape=jax.ShapeDtypeStruct((chunk_count * depth * rows, steps, LANES), jnp.float32),
-        in_specs=[pl.BlockSpec(memory_space=pltpu.SMEM), pl.BlockSpec(memory_space=pltpu.VMEM)],
+        in_specs=[pl.BlockSpec(memory_space=pltpu.SMEM)] * 3
+        + [pl.BlockSpec(memory_space=pltpu.VMEM)],
         out_specs=pl.BlockSpec(memory_space=pltpu.VMEM),
         compiler_params=pltpu.CompilerParams(vmem_limit_bytes=32 * 2**20),
-    )(places, tiles).reshape(chunk_count, depth, rows * steps, LANES)
+    )(spot_rows, lane_at, turns, tiles).reshape(chunk_count, depth, rows * steps, LANES)
 
     f32 = jnp.float32
     grid_shape = jax.ShapeDtypeStruct((depth, rows, length), f32)
     anywhere = pl.BlockSpec(memory_space=pl.ANY)
     cells = (chunk_count, depth, rows, LANES)
-    image, light, earlier, latest = pl.pallas_call(
-        functools.partial(wave_body, (steps, depth, rows, chunk_count)),
-        out_shape=[grid_shape] * 4,
+    shots = lax.axis_size("shot")
+    lines = 4 if shots % 4 == 0 else 1
+    columns = shots // lines
+    part = depth * (rows // shots)
+    shares = (columns, chunk_count, lines, part, LANES)
+    dma = pltpu.SemaphoreType.DMA
+    gradient, earlier, latest = pl.pallas_call(
+        functools.partial(wave_body, (steps, depth, rows, chunk_count, lines, columns)),
+        out_shape=[jax.ShapeDtypeStruct((chunk_count, part, LANES), f32)] + [grid_shape] * 2,
         in_specs=[anywhere] * 8 + [pl.BlockSpec(memory_space=pltpu.SMEM)],
-        out_specs=[anywhere] * 4,
+        out_specs=[pl.BlockSpec(memory_space=pltpu.VMEM)] + [anywhere] * 2,
         scratch_shapes=[
             pltpu.VMEM((2, chunk_count, depth + 2 * HALO, rows + 2 * PAD, LANES), f32),
             pltpu.VMEM(cells, f32),
@@ -370,16 +438,26 @@
             pltpu.VMEM(cells, f32),
             pltpu.VMEM(cells, f32),
             pltpu.VMEM(cells, f32),
-            pltpu.VMEM(cells, f32),
             pltpu.VMEM((steps, depth, rows, length), jnp.bfloat16),
             pltpu.VMEM((chunk_count, depth, rows * steps, LANES), f32),
             pltpu.VMEM((chunk_count, rows + 2 * PAD, LANES), f32),
-            pltpu.SemaphoreType.DMA((6 * chunk_count + 2,)),
-            pltpu.SemaphoreType.DMA((4 * chunk_count,)),
-            pltpu.SemaphoreType.DMA((2, chunk_count, 2)),
-            pltpu.SemaphoreType.DMA((2, chunk_count, 2)),
-            pltpu.SemaphoreType.DMA((2, chunk_count)),
-            pltpu.SemaphoreType.DMA((2, chunk_count)),
+            pltpu.VMEM(shares, f32),
+            pltpu.VMEM((shots - 1, chunk_count, part, LANES), f32),
+            pltpu.VMEM(shares, f32),
+            pltpu.VMEM((max(1, columns - 1),) + shares[1:], f32),
+            pltpu.VMEM((max(1, lines - 1), chunk_count, part, LANES), f32),
+            dma((6 * chunk_count + 2,)),
+            dma((2 * chunk_count,)),
+            dma((2, chunk_count, 2)),
+            dma((2, chunk_count, 2)),
+            dma((2, chunk_count)),
+            dma((2, chunk_count)),
+            dma((shots - 1,)),
+            dma((shots - 1,)),
+            dma((max(1, columns - 1), chunk_count)),
+            dma((max(1, columns - 1), chunk_count)),
+            dma((max(1, lines - 1), chunk_count)),
+            dma((max(1, lines - 1), chunk_count)),
         ],
         compiler_params=pltpu.CompilerParams(
             collective_id=0, has_side_effects=True, vmem_limit_bytes=48 * 2**20),
@@ -387,9 +465,8 @@
         stiffness, buoyancy_first, buoyancy_second, buoyancy_third, adjoint_before[0],
         adjoint_current[0], forward_field[0], dense, source_cell[0],
     )
-    summed_image = lax.psum_scatter(image.reshape(depth, -1), "shot", scatter_dimension=1, tiled=True)
-    summed_light = lax.psum_scatter(light.reshape(depth, -1), "shot", scatter_dimension=1, tiled=True)
-    gradient = summed_image / (summed_light / (steps * lax.axis_size("shot")) + DAMP)
+    gradient = gradient.reshape(chunk_count, depth, rows // shots, LANES)
+    gradient = gradient.transpose(1, 2, 0, 3).reshape(depth, -1)
     return (gradient, earlier[None], latest[None])
 
 

time: 245 us -> 114 us (0.47)
  waiting for transfers between devices: 125 us -> 0 us
  between operations: 14.1 us -> 0.79 us
  Pallas kernels: 78.3 us -> 88.1 us
    reduce_scatter x2 -> x0, waiting for transfers between devices: 125 us -> none  [the longest x1 65.8 us: local(): lax.psum_scatter(image.reshape(depth, -1), 'shot', scatter_dimension=1, t...]
    pallas_call x1, Pallas kernels: 63.9 us -> 78.5 us  [local(): pl.pallas_call(functools.partial(wave_body, (steps, depth, rows, chunk_co...]
    pallas_call x1, Pallas kernels: 14.3 us -> 9.69 us  [local(): pl.pallas_call(scatter_body, out_shape=jax.ShapeDtypeStruct((chunk_count...]
    unnamed x16 -> x18, local copies, waits for them, and re-layouts: 7.12 us -> 4.45 us
  transfers between devices with their start and end apart: 2 -> 0, of which waited for: 2 -> 0; matrix products, arithmetic and copies ran while one was open for 1% -> 0% of each run, Pallas kernels for 0% -> 0%
where the time goes in v2:
time: 114 us; the launch traced here: 113 us
  Pallas kernels  88.1 us (77%)
  blocking collectives  14.4 us (13%)
  local copies, waits for them, and re-layouts  5.78 us (5%)
  matrix products  2.34 us (2%)
  other arithmetic  1.79 us (2%)
    pallas_call x1, Pallas kernels, local(): pl.pallas_call(functools.partial(wave_body, (steps, depth, rows, chunk_co...  78.5 us
    all_to_all x1, blocking collectives, local(): lax.all_to_all(packed.reshape(device_count, capacity * (steps + 1)), ('sh...  14.4 us
    pallas_call x1, Pallas kernels, local(): pl.pallas_call(scatter_body, out_shape=jax.ShapeDtypeStruct((chunk_count...  9.69 us
    unnamed x18, local copies, waits for them, and re-layouts  4.45 us

profile of v2, /device:TPU:0, one launch (start us, length us, event | category | flops | bytes accessed | tf_op | source)
XLA Modules:
  0.0 113.2 jit_solution(5291703103816939523)
XLA Ops:
  0.6 0.0 copy-start
  0.7 1.0 fusion.1
  1.7 0.7 convert_add_fusion
  2.4 0.7 convert_element_type.20
  3.1 0.0 copy-done
  3.1 0.5 convolution_bitcast_fusion
  3.6 0.8 fusion
  4.4 0.2 all_to_all.8
  4.6 14.4 %all_to_all.10 = f32[32,1,216]{2,1,0:T(1,128)S(1)} all-to-all(f32[32,1,216]{2,1,0:T(1,128)S(1)} %all_to_all.8), channel_id=1, replica_groups=mesh['shot'=8,'sub'=4] {'shot','sub'}, dimensions={0} | all-to-all | bytes 55296 | tf_op jit(solution)/shard_map/all_to_all | solution.py:397
  19.0 0.1 reduce
  19.1 0.2 reshape.46
  19.2 0.3 fusion.4
  19.6 0.1 copy.24
  19.7 0.0 copy-start.2
  19.8 0.0 copy-start.3
  19.8 0.0 copy-start.4
  19.8 0.0 copy-start.5
  19.8 0.0 copy-start.6
  19.8 0.0 copy-start.7
  19.8 9.7 %shard_map.130 = f32[1536,8,128]{2,1,0:T(8,128)S(1)} custom-call(s32[768]{0:T(1024)S(1)} %get-tuple-element.11.row_ref, s32[768]{0:T(1024)S(1)} %get-tuple-element.10.at_ref, s32[768]{0:T(1024)S(1)} %get-tuple-element.9.turn_ref, f32[6,8,128]{2,1,0:T(8,128)S(1)} %bitcast.25), custom_call_target="tpu_custom_call" | custom-call | tf_op jit(solution)/shard_map/pallas_call | solution.py:409
  29.5 0.0 copy-start.1
  29.5 2.6 %copy-done.1 = f32[1536,8,128]{2,1,0:T(8,128)} copy-done((f32[1536,8,128]{2,1,0:T(8,128)}, f32[1536,8,128]{2,1,0:T(8,128)S(1)}, u32[]{:S(2)}) %copy-start.1) | copy-done | bytes 6291480
  32.2 0.0 copy-done.2
  32.2 0.0 copy-done.3
  32.2 0.0 copy-done.4
  32.2 0.0 copy-done.5
  32.2 0.0 copy-done.6
  32.2 0.0 copy-done.7
  32.2 78.5 %shard_map.131 = (f32[3,64,128]{2,1,0:T(8,128)S(1)}, f32[16,32,384]{2,1,0:T(8,128)S(1)}, f32[16,32,384]{2,1,0:T(8,128)S(1)}) custom-call(f32[16,32,384]{2,1,0:T(8,128)S(1)} %copy-done.2, f32[16,32,384]{2,1,0:T(8,128)S(1)} %copy-done.3, f32[16,32,384]{2,1,0:T(8,128)S(1)} %copy-done.4, f32[16,32,384]{2,1,0:T(8,128)S(1)} %copy-done.5, ...), custom_call_target="tpu_custom_call" | custom-call | tf_op jit(solution)/shard_map/pallas_call | solution.py:428
  110.7 0.1 copy.28
  110.7 0.7 reshape.50
  111.4 0.9 copy.31
  112.3 0.9 copy.32
  (3 shorter events, 0.1 us)
Async XLA Ops:
  0.6 2.4 %copy-start = (f32[512,256]{1,0:T(8,128)S(1)}, f32[512,256]{1,0:T(8,128)}, u32[]{:S(2)}) copy-start(f32[512,256]{1,0:T(8,128)} %param.18) | copy-start | bytes 1572868
  19.7 12.4 %copy-start.2 = (f32[16,32,384]{2,1,0:T(8,128)S(1)}, f32[16,32,384]{2,1,0:T(8,128)}, u32[]{:S(2)}) copy-start(f32[16,32,384]{2,1,0:T(8,128)} %stiff_hbm.1) | copy-start | bytes 2359300
  19.8 12.4 %copy-start.3 = (f32[16,32,384]{2,1,0:T(8,128)S(1)}, f32[16,32,384]{2,1,0:T(8,128)}, u32[]{:S(2)}) copy-start(f32[16,32,384]{2,1,0:T(8,128)} %first_hbm.1) | copy-start | bytes 2359300
  19.8 12.4 %copy-start.4 = (f32[16,32,384]{2,1,0:T(8,128)S(1)}, f32[16,32,384]{2,1,0:T(8,128)}, u32[]{:S(2)}) copy-start(f32[16,32,384]{2,1,0:T(8,128)} %second_hbm.1) | copy-start | bytes 2359300
  19.8 12.4 %copy-start.5 = (f32[16,32,384]{2,1,0:T(8,128)S(1)}, f32[16,32,384]{2,1,0:T(8,128)}, u32[]{:S(2)}) copy-start(f32[16,32,384]{2,1,0:T(8,128)} %third_hbm.1) | copy-start | bytes 2359300
  19.8 12.4 %copy-start.6 = (f32[1,16,32,384]{3,2,1,0:T(8,128)S(1)}, f32[1,16,32,384]{3,2,1,0:T(8,128)}, u32[]{:S(2)}) copy-start(f32[1,16,32,384]{3,2,1,0:T(8,128)} %param.15) | copy-start | bytes 2359300
  19.8 12.4 %copy-start.7 = (s32[1,3]{1,0:T(1,128)S(1)}, s32[1,3]{1,0:T(1,128)}, u32[]{:S(2)}) copy-start(s32[1,3]{1,0:T(1,128)} %param.21) | copy-start | bytes 40
  29.5 2.7 %copy-start.1 = (f32[1536,8,128]{2,1,0:T(8,128)}, f32[1536,8,128]{2,1,0:T(8,128)S(1)}, u32[]{:S(2)}) copy-start(f32[1536,8,128]{2,1,0:T(8,128)S(1)} %shard_map.130) | copy-start | bytes 18874372

commit v3 on v2

--- a/solution.py
+++ b/solution.py
@@ -49,6 +49,42 @@
     return out
 
 
+def exchange_body(shots, subs, mine_ref, got_ref, send_sem, recv_sem):
+    count = shots * subs
+    me = lax.axis_index("shot") * subs + lax.axis_index("sub")
+
+    def place(k):
+        to = lax.rem(me + k, count)
+        return {"shot": lax.div(to, subs), "sub": lax.rem(to, subs)}, to
+
+    barrier = pltpu.get_barrier_semaphore()
+
+    def greet(k, carry):
+        pl.semaphore_signal(barrier, inc=1, device_id=place(k)[0], device_id_type=MESH)
+        return carry
+
+    lax.fori_loop(1, count, greet, 0)
+    got_ref[count - 1] = mine_ref[me]
+    pl.semaphore_wait(barrier, count - 1)
+
+    def copy(k):
+        device, to = place(k)
+        return pltpu.make_async_remote_copy(
+            mine_ref.at[to], got_ref.at[k - 1], send_sem.at[k - 1], recv_sem.at[k - 1],
+            device_id=device, device_id_type=MESH)
+
+    def send(k, carry):
+        copy(k).start()
+        return carry
+
+    def finish(k, carry):
+        copy(k).wait()
+        return carry
+
+    lax.fori_loop(1, count, send, 0)
+    lax.fori_loop(1, count, finish, 0)
+
+
 def scatter_body(row_ref, at_ref, turn_ref, value_ref, dense_ref):
     dense_ref[...] = jnp.zeros_like(dense_ref)
     lane = lax.broadcasted_iota(jnp.int32, (8, LANES), 1)
@@ -56,14 +92,23 @@
     def block(group, carry):
         tile = value_ref[group]
 
-        def one(slot, inner):
-            number = group * LANES + slot
-            row = row_ref[number]
-            moved = pltpu.roll(tile, turn_ref[number], 1)
-            dense_ref[row] = dense_ref[row] + jnp.where(lane == at_ref[number], moved, 0.0)
+        def four(quad, inner):
+            spots, terms, found = [], [], []
+            for k in range(4):
+                number = group * LANES + quad * 4 + k
+                spots.append(row_ref[number])
+                moved = pltpu.roll(tile, turn_ref[number], 1)
+                terms.append(jnp.where(lane == at_ref[number], moved, 0.0))
+                found.append(dense_ref[spots[k]])
+            for k in range(4):
+                total = found[k] + terms[k]
+                for before in range(k):
+                    same = jnp.where(spots[before] == spots[k], 1.0, 0.0)
+                    total = total + terms[before] * same
+                dense_ref[spots[k]] = total
             return inner
 
-        return lax.fori_loop(0, LANES, one, carry, unroll=8)
+        return lax.fori_loop(0, LANES // 4, four, carry, unroll=4)
 
     lax.fori_loop(0, value_ref.shape[0], block, 0)
 
@@ -71,11 +116,11 @@
 def wave_body(
     dims,
     stiff_hbm, first_hbm, second_hbm, third_hbm, before_hbm, current_hbm, forward_hbm,
-    inject_hbm, source_ref,
+    left_hbm, right_hbm, inject, source_ref,
     gradient_out, earlier_out, latest_out,
-    field, stiff, first, second, third, partial, image, forward, inject, flux,
+    field, stiff, first, second, third, partial, image, forward, flux,
     light_blocks, light_got, image_blocks, image_got, image_last,
-    load_sem, store_sem, edge_send, edge_recv, face_send, face_recv,
+    load_sem, store_sem, edge_send, edge_recv,
     light_send, light_recv, across_send, across_recv, along_send, along_recv,
 ):
     steps, depth, rows, chunk_count, lines, columns = dims
@@ -99,8 +144,6 @@
         for plane in list(range(HALO)) + list(range(HALO + depth, 2 * HALO + depth)):
             for b in range(2):
                 field[b, c, plane] = jnp.zeros((2 * PAD + rows, LANES), jnp.float32)
-        for face in list(range(4)) + list(range(4 + depth, 7 + depth)):
-            first[c, face] = jnp.zeros((rows, LANES), jnp.float32)
         flux[c] = jnp.zeros((2 * PAD + rows, LANES), jnp.float32)
 
     barrier = pltpu.get_barrier_semaphore()
@@ -138,30 +181,19 @@
         load(first_hbm.at[:, :, lanes(c)], first.at[c, pl.ds(4, depth)])
         load(stiff_hbm.at[:, :, lanes(c)], stiff.at[c])
         load(before_hbm.at[:, :, lanes(c)], field.at[1, c, pl.ds(HALO, depth), inner, :])
-    load(inject_hbm, inject)
+    for c in range(chunk_count):
+        load(left_hbm.at[pl.ds(0, HALO), :, lanes(c)], field.at[0, c, pl.ds(0, HALO), inner, :])
+        load(left_hbm.at[pl.ds(HALO, 4), :, lanes(c)], first.at[c, pl.ds(0, 4)])
+        load(right_hbm.at[pl.ds(0, HALO), :, lanes(c)],
+             field.at[0, c, pl.ds(HALO + depth, HALO), inner, :])
+        load(right_hbm.at[pl.ds(HALO, 3), :, lanes(c)], first.at[c, pl.ds(4 + depth, 3)])
 
     pl.semaphore_wait(
         barrier, (shots - 1) + jnp.where(has_left, 1, 0) + jnp.where(has_right, 1, 0))
 
-    def face_copy(side, c):
-        if side == 0:
-            src = first_hbm.at[pl.ds(0, 3), :, lanes(c)]
-            dst = first.at[c, pl.ds(4 + depth, 3)]
-            to = sub - 1
-        else:
-            src = first_hbm.at[pl.ds(depth - 4, 4), :, lanes(c)]
-            dst = first.at[c, pl.ds(0, 4)]
-            to = sub + 1
-        return pltpu.make_async_remote_copy(
-            src, dst, face_send.at[side, c], face_recv.at[side, c],
-            device_id={"sub": to}, device_id_type=MESH)
-
-    def edge_copy(side, c, b, from_hbm=False):
+    def edge_copy(side, c, b):
         start = 0 if side == 0 else depth - HALO
-        if from_hbm:
-            src = current_hbm.at[pl.ds(start, HALO), :, lanes(c)]
-        else:
-            src = field.at[b, c, pl.ds(HALO + start, HALO), inner, :]
+        src = field.at[b, c, pl.ds(HALO + start, HALO), inner, :]
         dst = field.at[b, c, pl.ds(HALO + depth if side == 0 else 0, HALO), inner, :]
         return pltpu.make_async_remote_copy(
             src, dst, edge_send.at[side, c, b], edge_recv.at[side, c, b],
@@ -169,13 +201,6 @@
 
     sends_on = (has_left, has_right)
     gets_on = (has_right, has_left)
-    for c in range(chunk_count):
-        for side in range(2):
-            @pl.when(sends_on[side])
-            def _(side=side, c=c):
-                edge_copy(side, c, 0, True).start()
-                face_copy(side, c).start()
-
     lane = lax.broadcasted_iota(jnp.int32, (8, LANES), 1)
     base = PAD + lax.div(sub, lax.axis_size("sub"))
     for copy in loads[:early]:
@@ -269,16 +294,6 @@
             image_blocks, c, x, image[c, x] * (1.0 - jnp.exp(-distance / (2.0 * MUTE * MUTE))))
         return carry
 
-    for c in range(chunk_count):
-        for side in range(2):
-            @pl.when(gets_on[side])
-            def _(side=side, c=c):
-                face_copy(side, c).wait_recv()
-
-            @pl.when(sends_on[side])
-            def _(side=side, c=c):
-                face_copy(side, c).wait_send()
-
     def outer_part(c, t, b, half, carry):
         y = pl.multiple_of(half * 16, 16)
         at = pl.ds(y, 16)
@@ -310,11 +325,11 @@
 
         for c in range(chunk_count):
             for side in range(2):
-                @pl.when(gets_on[side])
+                @pl.when(jnp.logical_and(gets_on[side], t > 0))
                 def _(side=side, c=c):
                     edge_copy(side, c, b).wait_recv()
 
-                @pl.when(sends_on[side])
+                @pl.when(jnp.logical_and(sends_on[side], t > 0))
                 def _(side=side, c=c):
                     edge_copy(side, c, b).wait_send()
 
@@ -345,23 +360,25 @@
         store(field.at[(steps - 1) % 2, c, body, inner, :], earlier_out.at[:, :, lanes(c)])
         store(field.at[steps % 2, c, body, inner, :], latest_out.at[:, :, lanes(c)])
 
+    for k in range(1, shots):
+        light_copy(k).wait()
+    for c in range(chunk_count):
+        light = light_blocks[column, c, line]
+        for k in range(1, shots):
+            light = light + light_got[k - 1, c]
+        light_blocks[column, c, line] = light / (steps * shots) + DAMP
     for c in range(chunk_count):
         for k in range(1, columns):
             across_copy(k, c).wait()
             image_blocks[column, c] = image_blocks[column, c] + image_got[k - 1, c]
         for k in range(1, lines):
             along_copy(k, c).start()
-    for k in range(1, shots):
-        light_copy(k).wait()
-    for c in range(chunk_count):
-        light = light_blocks[column, c, line]
-        for k in range(1, shots):
-            light = light + light_got[k - 1, c]
+    for c in range(chunk_count):
         summed = image_blocks[column, c, line]
         for k in range(1, lines):
             along_copy(k, c).wait()
             summed = summed + image_last[k - 1, c]
-        gradient_out[c] = summed / (light / (steps * shots) + DAMP)
+        gradient_out[c] = summed / light_blocks[column, c, line]
     for copy in stores:
         copy.wait()
 
@@ -378,6 +395,15 @@
     row_count = traces.shape[0]
     capacity = max(2, (3 * row_count + 2 * device_count - 1) // (2 * device_count))
     slots = device_count * capacity
+
+    subs = lax.axis_size("sub")
+    rightward = [(i, i + 1) for i in range(subs - 1)]
+    leftward = [(i + 1, i) for i in range(subs - 1)]
+    left_halo = lax.ppermute(
+        jnp.concatenate([adjoint_current[0, depth - HALO:], buoyancy_first[depth - 4:]], axis=0),
+        "sub", rightward)
+    right_halo = lax.ppermute(
+        jnp.concatenate([adjoint_current[0, :HALO], buoyancy_first[:3]], axis=0), "sub", leftward)
 
     kernel = trace_kernel(sample_count, steps)
     values = jnp.dot(
@@ -394,9 +420,20 @@
     rows_out = jnp.concatenate([values, receiver_cell.astype(jnp.float32)[:, None]], axis=1)
     packed = jnp.dot(
         chosen, rows_out, precision=lax.Precision.HIGHEST, preferred_element_type=jnp.float32)
-    got = lax.all_to_all(
-        packed.reshape(device_count, capacity * (steps + 1)), ("shot", "sub"),
-        split_axis=0, concat_axis=0, tiled=True).reshape(slots, steps + 1)
+    words = capacity * (steps + 1)
+    lines_out = -(-words // LANES)
+    mine = jnp.pad(packed.reshape(device_count, words), ((0, 0), (0, lines_out * LANES - words)))
+    dma = pltpu.SemaphoreType.DMA
+    in_vmem = pl.BlockSpec(memory_space=pltpu.VMEM)
+    got = pl.pallas_call(
+        functools.partial(exchange_body, lax.axis_size("shot"), lax.axis_size("sub")),
+        out_shape=jax.ShapeDtypeStruct((device_count, lines_out, LANES), jnp.float32),
+        in_specs=[in_vmem],
+        out_specs=in_vmem,
+        scratch_shapes=[dma((device_count - 1,)), dma((device_count - 1,))],
+        compiler_params=pltpu.CompilerParams(collective_id=1, has_side_effects=True),
+    )(mine.reshape(device_count, lines_out, LANES))
+    got = got.reshape(device_count, -1)[:, :words].reshape(slots, steps + 1)
     groups = -(-slots // LANES)
     got = jnp.pad(got, ((0, groups * LANES - slots), (0, 0)))
     places = (got[:, steps] + 0.5).astype(jnp.int32)
@@ -412,7 +449,9 @@
         in_specs=[pl.BlockSpec(memory_space=pltpu.SMEM)] * 3
         + [pl.BlockSpec(memory_space=pltpu.VMEM)],
         out_specs=pl.BlockSpec(memory_space=pltpu.VMEM),
-        compiler_params=pltpu.CompilerParams(vmem_limit_bytes=32 * 2**20),
+        cost_estimate=pl.CostEstimate(
+            flops=16 * slots * steps * LANES, bytes_accessed=2**25, transcendentals=0),
+        compiler_params=pltpu.CompilerParams(vmem_limit_bytes=14 * 2**20),
     )(spot_rows, lane_at, turns, tiles).reshape(chunk_count, depth, rows * steps, LANES)
 
     f32 = jnp.float32
@@ -424,11 +463,10 @@
     columns = shots // lines
     part = depth * (rows // shots)
     shares = (columns, chunk_count, lines, part, LANES)
-    dma = pltpu.SemaphoreType.DMA
     gradient, earlier, latest = pl.pallas_call(
         functools.partial(wave_body, (steps, depth, rows, chunk_count, lines, columns)),
         out_shape=[jax.ShapeDtypeStruct((chunk_count, part, LANES), f32)] + [grid_shape] * 2,
-        in_specs=[anywhere] * 8 + [pl.BlockSpec(memory_space=pltpu.SMEM)],
+        in_specs=[anywhere] * 9 + [in_vmem, pl.BlockSpec(memory_space=pltpu.SMEM)],
         out_specs=[pl.BlockSpec(memory_space=pltpu.VMEM)] + [anywhere] * 2,
         scratch_shapes=[
             pltpu.VMEM((2, chunk_count, depth + 2 * HALO, rows + 2 * PAD, LANES), f32),
@@ -439,19 +477,16 @@
             pltpu.VMEM(cells, f32),
             pltpu.VMEM(cells, f32),
             pltpu.VMEM((steps, depth, rows, length), jnp.bfloat16),
-            pltpu.VMEM((chunk_count, depth, rows * steps, LANES), f32),
             pltpu.VMEM((chunk_count, rows + 2 * PAD, LANES), f32),
             pltpu.VMEM(shares, f32),
             pltpu.VMEM((shots - 1, chunk_count, part, LANES), f32),
             pltpu.VMEM(shares, f32),
             pltpu.VMEM((max(1, columns - 1),) + shares[1:], f32),
             pltpu.VMEM((max(1, lines - 1), chunk_count, part, LANES), f32),
-            dma((6 * chunk_count + 2,)),
+            dma((10 * chunk_count + 1,)),
             dma((2 * chunk_count,)),
             dma((2, chunk_count, 2)),
             dma((2, chunk_count, 2)),
-            dma((2, chunk_count)),
-            dma((2, chunk_count)),
             dma((shots - 1,)),
             dma((shots - 1,)),
             dma((max(1, columns - 1), chunk_count)),
@@ -460,10 +495,10 @@
             dma((max(1, lines - 1), chunk_count)),
         ],
         compiler_params=pltpu.CompilerParams(
-            collective_id=0, has_side_effects=True, vmem_limit_bytes=48 * 2**20),
+            collective_id=0, has_side_effects=True, vmem_limit_bytes=26 * 2**20),
     )(
         stiffness, buoyancy_first, buoyancy_second, buoyancy_third, adjoint_before[0],
-        adjoint_current[0], forward_field[0], dense, source_cell[0],
+        adjoint_current[0], forward_field[0], left_halo, right_halo, dense, source_cell[0],
     )
     gradient = gradient.reshape(chunk_count, depth, rows // shots, LANES)
     gradient = gradient.transpose(1, 2, 0, 3).reshape(depth, -1)

time: 114 us -> 116 us (1.018)
  blocking collectives: 14.4 us -> 0 us
  Pallas kernels: 88.1 us -> 97 us
  starting transfers between devices: 0 us -> 4.33 us
  local copies, waits for them, and re-layouts: 5.78 us -> 9.52 us
    all_to_all x1 -> x0, blocking collectives: 14.4 us -> none  [local(): lax.all_to_all(packed.reshape(device_count, capacity * (steps + 1)), ('sh...]
    pallas_call x0 -> x1, Pallas kernels: none -> 12 us  [local(): pl.pallas_call(functools.partial(exchange_body, lax.axis_size('shot'), la...]
    ppermute x0 -> x2, starting transfers between devices: none -> 4.33 us  [the longest x1 3.05 us: local(): lax.ppermute(jnp.concatenate([adjoint_current[0, depth - HALO:], buoyancy...]
    pallas_call x1, Pallas kernels: 9.69 us -> 6.12 us  [local(): pl.pallas_call(scatter_body, out_shape=jax.ShapeDtypeStruct((chunk_count...]
    concatenate x0 -> x2, other arithmetic: none -> 1.65 us  [the longest x1 0.84 us: local(): jnp.concatenate([adjoint_current[0, depth - HALO:], buoyancy_first[depth...]
    unnamed x18 -> x29, local copies, waits for them, and re-layouts: 4.45 us -> 5.51 us
  transfers between devices with their start and end apart: 0 -> 2, of which waited for: 0 -> 0; matrix products, arithmetic and copies ran while one was open for 0% -> 4% of each run, Pallas kernels for 0% -> 16%
where the time goes in v3:
time: 116 us; the launch traced here: 115 us
  Pallas kernels  97 us (84%)
  local copies, waits for them, and re-layouts  9.52 us (8%)
  starting transfers between devices  4.33 us (4%)
  other arithmetic  2 us (2%)
  matrix products  1.58 us (1%)
    pallas_call x1, Pallas kernels, local(): pl.pallas_call(functools.partial(wave_body, (steps, depth, rows, chunk_co...  78.9 us
    pallas_call x1, Pallas kernels, local(): pl.pallas_call(functools.partial(exchange_body, lax.axis_size('shot'), la...  12 us
    pallas_call x1, Pallas kernels, local(): pl.pallas_call(scatter_body, out_shape=jax.ShapeDtypeStruct((chunk_count...  6.12 us
    unnamed x29, local copies, waits for them, and re-layouts  5.51 us
    ppermute x1, starting transfers between devices, local(): lax.ppermute(jnp.concatenate([adjoint_current[0, depth - HALO:], buoyancy...  3.05 us
  transfers between devices with their start and end apart: 2, of which 0 were waited for; matrix products, arithmetic and copies ran while one was open for 4% of the time, Pallas kernels for 16%

profile of v3, /device:TPU:0, one launch (start us, length us, event | category | flops | bytes accessed | tf_op | source)
XLA Modules:
  0.0 115.4 jit_solution(13239211673630707184)
XLA Ops:
  0.6 0.0 copy-start
  0.6 0.0 slice-start
  0.7 0.0 copy-start.11
  0.7 0.0 copy-start.12
  0.7 1.0 slice.24
  1.7 1.1 slice_bitcast_fusion.1
  2.8 0.8 pad_maximum_fusion.1
  3.6 1.3 %collective-permute-start.1 = (f32[10,32,384]{2,1,0:T(8,128)}, f32[10,32,384]{2,1,0:T(8,128)S(1)}, u32[]{:S(2)}, u32[]{:S(2)}) collective-permute-start(f32[10,32,384]{2,1,0:T(8,128)} %pad_maximum_fusion.1), channel_id=1, source_target_pairs={{1,0},{2,1},{3,2},{5,4},{6,5},{7,6},{9,8},{10,9},{11,10},{13,12},{... | collective-permute-start | bytes 1474568 | tf_op jit(solution)/shard_map/ppermute | solution.py:405
  4.9 0.0 slice-done
  4.9 0.8 pad_maximum_fusion
  5.8 3.1 %collective-permute-start = (f32[11,32,384]{2,1,0:T(8,128)}, f32[11,32,384]{2,1,0:T(8,128)S(1)}, u32[]{:S(2)}, u32[]{:S(2)}) collective-permute-start(f32[11,32,384]{2,1,0:T(8,128)} %pad_maximum_fusion), channel_id=1, source_target_pairs={{0,1},{1,2},{2,3},{4,5},{5,6},{6,7},{8,9},{9,10},{10,11},{12,13},{... | collective-permute-start | bytes 1622024 | tf_op jit(solution)/shard_map/ppermute | solution.py:402
  8.8 0.0 copy-done.11
  8.8 0.3 fusion.1
  9.1 0.0 copy-done.12
  9.1 0.0 copy-done
  9.2 0.5 convolution_bitcast_fusion
  9.7 0.8 fusion
  10.5 0.2 reshape.50
  10.7 0.6 reshape.51.mine_ref
  11.3 12.0 %shard_map.130 = f32[32,2,128]{2,1,0:T(2,128)} custom-call(f32[32,2,128]{2,1,0:T(2,128)} %reshape.51.mine_ref), custom_call_target="tpu_custom_call" | custom-call | tf_op jit(solution)/shard_map/pallas_call | solution.py:428
  23.3 0.8 copy.29
  24.0 0.2 reshape.53
  24.3 0.0 copy-start.6
  24.3 0.1 copy.22
  24.4 0.3 fusion.4
  24.7 0.0 copy-start.1
  24.7 0.0 copy-start.2
  24.8 0.0 copy-start.3
  24.8 0.0 copy-start.4
  24.8 0.0 copy-start.5
  24.8 0.0 copy-start.10
  24.8 6.1 %shard_map.131 = f32[1536,8,128]{2,1,0:T(8,128)S(1)} custom-call(s32[768]{0:T(1024)S(1)} %get-tuple-element.13.row_ref, s32[768]{0:T(1024)S(1)} %get-tuple-element.12.at_ref, s32[768]{0:T(1024)S(1)} %get-tuple-element.11.turn_ref, f32[6,8,128]{2,1,0:T(8,128)S(1)} %bitcast.36), custom_call_target="tpu_custom_call" | custom-call | flops 12582912 | bytes 33554432 | tf_op jit(solution)/shard_map/pallas_call | solution.py:446
  30.9 0.0 collective-permute-done.1.right_hbm
  30.9 0.0 copy-start.8
  31.0 0.8 copy-done.8
  31.7 0.0 collective-permute-done.left_hbm
  31.7 0.0 copy-done.6
  31.7 0.0 copy-done.1
  31.7 0.0 copy-done.2
  31.7 0.0 copy-done.3
  31.8 0.0 copy-start.7
  31.8 1.1 copy-done.7
  32.9 1.0 copy-done.9
  34.0 78.9 %shard_map.132 = (f32[3,64,128]{2,1,0:T(8,128)S(1)}, f32[16,32,384]{2,1,0:T(8,128)S(1)}, f32[16,32,384]{2,1,0:T(8,128)S(1)}) custom-call(f32[16,32,384]{2,1,0:T(8,128)S(1)} %copy-done.4, f32[16,32,384]{2,1,0:T(8,128)S(1)} %copy-done.3, f32[16,32,384]{2,1,0:T(8,128)S(1)} %copy-done.5, f32[16,32,384]{2,1,0:T(8,128)S(1)} %copy-done.6, ...), custom_call_target="tpu_custom_call" | custom-call | tf_op jit(solution)/shard_map/pallas_call | solution.py:466
  112.8 0.1 copy.28
  112.9 0.7 reshape.57
  113.6 0.9 copy.32
  114.5 0.9 copy.33
  (10 shorter events, 0.1 us)
Async XLA Ops:
  0.6 8.5 %copy-start = (f32[512,256]{1,0:T(8,128)S(1)}, f32[512,256]{1,0:T(8,128)}, u32[]{:S(2)}) copy-start(f32[512,256]{1,0:T(8,128)} %param.18) | copy-start | bytes 1572868
  0.6 4.3 %slice-start = ((f32[16,32,384]{2,1,0:T(8,128)}), f32[4,32,384]{2,1,0:T(8,128)S(1)}, s32[]{:S(2)}) async-start(f32[16,32,384]{2,1,0:T(8,128)} %first_hbm.1), calls=%async_computation | async-start | bytes 393216 | tf_op jit(solution)/shard_map/slice | solution.py:403
  0.7 8.2 %copy-start.11 = (s32[512,1]{0,1:T(1,128)S(1)}, s32[512,1]{0,1:T(1,128)}, u32[]{:S(2)}) copy-start(s32[512,1]{0,1:T(1,128)} %param.19) | copy-start | bytes 6148
  0.7 8.5 %copy-start.12 = (s32[512]{0:T(512)S(1)}, s32[512]{0:T(512)}, u32[]{:S(2)}) copy-start(s32[512]{0:T(512)} %param.20) | copy-start | bytes 6148
  3.6 27.3 %collective-permute-start.1 = (f32[10,32,384]{2,1,0:T(8,128)}, f32[10,32,384]{2,1,0:T(8,128)S(1)}, u32[]{:S(2)}, u32[]{:S(2)}) collective-permute-start(f32[10,32,384]{2,1,0:T(8,128)} %pad_maximum_fusion.1), channel_id=1, source_target_pairs={{1,0},{2,1},{3,2},{5,4},{6,5},{7,6},{9,8},{10,9},{11,10},{13,12},{... | collective-permute-start | bytes 1474568 | tf_op jit(solution)/shard_map/ppermute | solution.py:405
  5.8 26.0 %collective-permute-start = (f32[11,32,384]{2,1,0:T(8,128)}, f32[11,32,384]{2,1,0:T(8,128)S(1)}, u32[]{:S(2)}, u32[]{:S(2)}) collective-permute-start(f32[11,32,384]{2,1,0:T(8,128)} %pad_maximum_fusion), channel_id=1, source_target_pairs={{0,1},{1,2},{2,3},{4,5},{5,6},{6,7},{8,9},{9,10},{10,11},{12,13},{... | collective-permute-start | bytes 1622024 | tf_op jit(solution)/shard_map/ppermute | solution.py:402
  24.3 7.5 %copy-start.6 = (f32[16,32,384]{2,1,0:T(8,128)S(1)}, f32[16,32,384]{2,1,0:T(8,128)}, u32[]{:S(2)}) copy-start(f32[16,32,384]{2,1,0:T(8,128)} %third_hbm.1) | copy-start | bytes 2359300
  24.7 7.0 %copy-start.1 = (bf16[1,8,16,32,384]{4,3,2,1,0:T(8,128)(2,1)S(1)}, bf16[1,8,16,32,384]{4,3,2,1,0:T(8,128)(2,1)}, u32[]{:S(2)}) copy-start(bf16[1,8,16,32,384]{4,3,2,1,0:T(8,128)(2,1)} %param.17) | copy-start | bytes 9437188
  24.7 7.0 %copy-start.2 = (f32[1,16,32,384]{3,2,1,0:T(8,128)S(1)}, f32[1,16,32,384]{3,2,1,0:T(8,128)}, u32[]{:S(2)}) copy-start(f32[1,16,32,384]{3,2,1,0:T(8,128)} %param.16) | copy-start | bytes 2359300
  24.8 7.0 %copy-start.3 = (f32[16,32,384]{2,1,0:T(8,128)S(1)}, f32[16,32,384]{2,1,0:T(8,128)}, u32[]{:S(2)}) copy-start(f32[16,32,384]{2,1,0:T(8,128)} %first_hbm.1) | copy-start | bytes 2359300
  24.8 7.0 %copy-start.4 = (f32[16,32,384]{2,1,0:T(8,128)S(1)}, f32[16,32,384]{2,1,0:T(8,128)}, u32[]{:S(2)}) copy-start(f32[16,32,384]{2,1,0:T(8,128)} %stiff_hbm.1) | copy-start | bytes 2359300
  24.8 7.0 %copy-start.5 = (f32[16,32,384]{2,1,0:T(8,128)S(1)}, f32[16,32,384]{2,1,0:T(8,128)}, u32[]{:S(2)}) copy-start(f32[16,32,384]{2,1,0:T(8,128)} %second_hbm.1) | copy-start | bytes 2359300
  24.8 7.0 %copy-start.10 = (s32[1,3]{1,0:T(1,128)S(1)}, s32[1,3]{1,0:T(1,128)}, u32[]{:S(2)}) copy-start(s32[1,3]{1,0:T(1,128)} %param.21) | copy-start | bytes 40
  30.9 0.8 copy-start.8
  31.8 1.1 copy-start.7
  32.9 1.0 copy-start.9

commit v4 on v3

--- a/solution.py
+++ b/solution.py
@@ -31,22 +31,6 @@
     for ratio, (ahead, behind) in zip(RATIOS[1:], pairs[1:]):
         total = total + ratio * (ahead - behind)
     return total
-
-
-def shifted(chunks, amount, lane):
-    if amount == 0:
-        return chunks
-    rolled = [pltpu.roll(chunk, (-amount) % LANES, 1) for chunk in chunks]
-    zero = jnp.zeros_like(chunks[0])
-    out = []
-    for c in range(len(chunks)):
-        if amount > 0:
-            other = rolled[c + 1] if c + 1 < len(chunks) else zero
-            out.append(jnp.where(lane < LANES - amount, rolled[c], other))
-        else:
-            other = rolled[c - 1] if c > 0 else zero
-            out.append(jnp.where(lane >= -amount, rolled[c], other))
-    return out
 
 
 def exchange_body(shots, subs, mine_ref, got_ref, send_sem, recv_sem):
@@ -116,11 +100,12 @@
 def wave_body(
     dims,
     stiff_hbm, first_hbm, second_hbm, third_hbm, before_hbm, current_hbm, forward_hbm,
-    left_hbm, right_hbm, inject, source_ref,
+    inject, source_ref,
     gradient_out, earlier_out, latest_out,
     field, stiff, first, second, third, partial, image, forward, flux,
+    turned, flux_turned, third_turned,
     light_blocks, light_got, image_blocks, image_got, image_last,
-    load_sem, store_sem, edge_send, edge_recv,
+    load_sem, store_sem, edge_send, edge_recv, face_send, face_recv,
     light_send, light_recv, across_send, across_recv, along_send, along_recv,
 ):
     steps, depth, rows, chunk_count, lines, columns = dims
@@ -144,6 +129,8 @@
         for plane in list(range(HALO)) + list(range(HALO + depth, 2 * HALO + depth)):
             for b in range(2):
                 field[b, c, plane] = jnp.zeros((2 * PAD + rows, LANES), jnp.float32)
+        for face in list(range(4)) + list(range(4 + depth, 7 + depth)):
+            first[c, face] = jnp.zeros((rows, LANES), jnp.float32)
         flux[c] = jnp.zeros((2 * PAD + rows, LANES), jnp.float32)
 
     barrier = pltpu.get_barrier_semaphore()
@@ -181,19 +168,28 @@
         load(first_hbm.at[:, :, lanes(c)], first.at[c, pl.ds(4, depth)])
         load(stiff_hbm.at[:, :, lanes(c)], stiff.at[c])
         load(before_hbm.at[:, :, lanes(c)], field.at[1, c, pl.ds(HALO, depth), inner, :])
-    for c in range(chunk_count):
-        load(left_hbm.at[pl.ds(0, HALO), :, lanes(c)], field.at[0, c, pl.ds(0, HALO), inner, :])
-        load(left_hbm.at[pl.ds(HALO, 4), :, lanes(c)], first.at[c, pl.ds(0, 4)])
-        load(right_hbm.at[pl.ds(0, HALO), :, lanes(c)],
-             field.at[0, c, pl.ds(HALO + depth, HALO), inner, :])
-        load(right_hbm.at[pl.ds(HALO, 3), :, lanes(c)], first.at[c, pl.ds(4 + depth, 3)])
-
     pl.semaphore_wait(
         barrier, (shots - 1) + jnp.where(has_left, 1, 0) + jnp.where(has_right, 1, 0))
 
-    def edge_copy(side, c, b):
+    def face_copy(side, c):
+        if side == 0:
+            src = first_hbm.at[pl.ds(0, 3), :, lanes(c)]
+            dst = first.at[c, pl.ds(4 + depth, 3)]
+            to = sub - 1
+        else:
+            src = first_hbm.at[pl.ds(depth - 4, 4), :, lanes(c)]
+            dst = first.at[c, pl.ds(0, 4)]
+            to = sub + 1
+        return pltpu.make_async_remote_copy(
+            src, dst, face_send.at[side, c], face_recv.at[side, c],
+            device_id={"sub": to}, device_id_type=MESH)
+
+    def edge_copy(side, c, b, from_hbm=False):
         start = 0 if side == 0 else depth - HALO
-        src = field.at[b, c, pl.ds(HALO + start, HALO), inner, :]
+        if from_hbm:
+            src = current_hbm.at[pl.ds(start, HALO), :, lanes(c)]
+        else:
+            src = field.at[b, c, pl.ds(HALO + start, HALO), inner, :]
         dst = field.at[b, c, pl.ds(HALO + depth if side == 0 else 0, HALO), inner, :]
         return pltpu.make_async_remote_copy(
             src, dst, edge_send.at[side, c, b], edge_recv.at[side, c, b],
@@ -201,23 +197,57 @@
 
     sends_on = (has_left, has_right)
     gets_on = (has_right, has_left)
-    lane = lax.broadcasted_iota(jnp.int32, (8, LANES), 1)
+    for c in range(chunk_count):
+        for side in range(2):
+            @pl.when(sends_on[side])
+            def _(side=side, c=c):
+                edge_copy(side, c, 0, True).start()
+                face_copy(side, c).start()
     base = PAD + lax.div(sub, lax.axis_size("sub"))
     for copy in loads[:early]:
         copy.wait()
 
+    planes = LANES // rows
+    tall = chunk_count * LANES
+
+    def turn(tile):
+        return tile.reshape(LANES, LANES).T
+
+    def turn_faces(g, carry):
+        for c in range(chunk_count):
+            third_turned[g, c * LANES:(c + 1) * LANES, :] = turn(
+                third[c, pl.ds(g * planes, planes)])
+        return carry
+
+    def third_part(b, g, carry):
+        for c in range(chunk_count):
+            turned[PAD + c * LANES:PAD + (c + 1) * LANES, :] = turn(
+                field[b, c, pl.ds(HALO + g * planes, planes), PAD:PAD + rows, :])
+
+        def out(i, inside):
+            def near(s):
+                return turned[pl.ds(PAD + i * 8 + s, 8), :]
+            flux_turned[pl.ds(pl.multiple_of(PAD + i * 8, 8), 8), :] = (
+                third_turned[g, pl.ds(pl.multiple_of(i * 8, 8), 8), :]
+                * weighted([(near(k), near(1 - k)) for k in range(1, 5)]))
+            return inside
+
+        lax.fori_loop(0, tall // 8, out, 0, unroll=8)
+
+        def back(i, inside):
+            def near(s):
+                return flux_turned[pl.ds(PAD + i * 8 + s, 8), :]
+            turned[pl.ds(pl.multiple_of(PAD + i * 8, 8), 8), :] = weighted(
+                [(near(k - 1), near(-k)) for k in range(1, 5)])
+            return inside
+
+        lax.fori_loop(0, tall // 8, back, 0, unroll=8)
+        for c in range(chunk_count):
+            partial[c, pl.ds(g * planes, planes)] = (
+                turned[PAD + c * LANES:PAD + (c + 1) * LANES, :].T.reshape(planes, rows, LANES))
+        return carry
+
     def inner_part(b, x, carry):
-        for y in range(0, rows, 8):
-            at = pl.ds(y, 8)
-            p = [field[b, c, HALO + x, pl.ds(PAD + y, 8), :] for c in range(chunk_count)]
-            pairs = [(shifted(p, k, lane), shifted(p, 1 - k, lane)) for k in range(1, 5)]
-            q = [
-                third[c, x, at, :] * weighted([(a[c], z[c]) for a, z in pairs])
-                for c in range(chunk_count)
-            ]
-            pairs = [(shifted(q, k - 1, lane), shifted(q, -k, lane)) for k in range(1, 5)]
-            for c in range(chunk_count):
-                partial[c, x, at, :] = weighted([(a[c], z[c]) for a, z in pairs])
         for c in range(chunk_count):
             for y in range(0, rows, 8):
                 def near(s, c=c, y=y):
@@ -234,8 +264,13 @@
         return carry
 
     def inner_all(b):
+        lax.fori_loop(0, depth // planes, functools.partial(third_part, b), 0)
         lax.fori_loop(0, depth, functools.partial(inner_part, b), 0)
 
+    for start in (0, PAD + tall):
+        turned[start:start + PAD, :] = zero_tile
+        flux_turned[start:start + PAD, :] = zero_tile
+    lax.fori_loop(0, depth // planes, turn_faces, 0)
     inner_all(0)
     for copy in loads[early:]:
         copy.wait()
@@ -293,6 +328,16 @@
         put_blocks(
             image_blocks, c, x, image[c, x] * (1.0 - jnp.exp(-distance / (2.0 * MUTE * MUTE))))
         return carry
+
+    for c in range(chunk_count):
+        for side in range(2):
+            @pl.when(gets_on[side])
+            def _(side=side, c=c):
+                face_copy(side, c).wait_recv()
+
+            @pl.when(sends_on[side])
+            def _(side=side, c=c):
+                face_copy(side, c).wait_send()
 
     def outer_part(c, t, b, half, carry):
         y = pl.multiple_of(half * 16, 16)
@@ -325,11 +370,11 @@
 
         for c in range(chunk_count):
             for side in range(2):
-                @pl.when(jnp.logical_and(gets_on[side], t > 0))
+                @pl.when(gets_on[side])
                 def _(side=side, c=c):
                     edge_copy(side, c, b).wait_recv()
 
-                @pl.when(jnp.logical_and(sends_on[side], t > 0))
+                @pl.when(sends_on[side])
                 def _(side=side, c=c):
                     edge_copy(side, c, b).wait_send()
 
@@ -395,15 +440,6 @@
     row_count = traces.shape[0]
     capacity = max(2, (3 * row_count + 2 * device_count - 1) // (2 * device_count))
     slots = device_count * capacity
-
-    subs = lax.axis_size("sub")
-    rightward = [(i, i + 1) for i in range(subs - 1)]
-    leftward = [(i + 1, i) for i in range(subs - 1)]
-    left_halo = lax.ppermute(
-        jnp.concatenate([adjoint_current[0, depth - HALO:], buoyancy_first[depth - 4:]], axis=0),
-        "sub", rightward)
-    right_halo = lax.ppermute(
-        jnp.concatenate([adjoint_current[0, :HALO], buoyancy_first[:3]], axis=0), "sub", leftward)
 
     kernel = trace_kernel(sample_count, steps)
     values = jnp.dot(
@@ -466,7 +502,7 @@
     gradient, earlier, latest = pl.pallas_call(
         functools.partial(wave_body, (steps, depth, rows, chunk_count, lines, columns)),
         out_shape=[jax.ShapeDtypeStruct((chunk_count, part, LANES), f32)] + [grid_shape] * 2,
-        in_specs=[anywhere] * 9 + [in_vmem, pl.BlockSpec(memory_space=pltpu.SMEM)],
+        in_specs=[anywhere] * 7 + [in_vmem, pl.BlockSpec(memory_space=pltpu.SMEM)],
         out_specs=[pl.BlockSpec(memory_space=pltpu.VMEM)] + [anywhere] * 2,
         scratch_shapes=[
             pltpu.VMEM((2, chunk_count, depth + 2 * HALO, rows + 2 * PAD, LANES), f32),
@@ -478,15 +514,20 @@
             pltpu.VMEM(cells, f32),
             pltpu.VMEM((steps, depth, rows, length), jnp.bfloat16),
             pltpu.VMEM((chunk_count, rows + 2 * PAD, LANES), f32),
+            pltpu.VMEM((length + 2 * PAD, LANES), f32),
+            pltpu.VMEM((length + 2 * PAD, LANES), f32),
+            pltpu.VMEM((depth * rows // LANES, length, LANES), f32),
             pltpu.VMEM(shares, f32),
             pltpu.VMEM((shots - 1, chunk_count, part, LANES), f32),
             pltpu.VMEM(shares, f32),
             pltpu.VMEM((max(1, columns - 1),) + shares[1:], f32),
             pltpu.VMEM((max(1, lines - 1), chunk_count, part, LANES), f32),
-            dma((10 * chunk_count + 1,)),
+            dma((6 * chunk_count + 1,)),
             dma((2 * chunk_count,)),
             dma((2, chunk_count, 2)),
             dma((2, chunk_count, 2)),
+            dma((2, chunk_count)),
+            dma((2, chunk_count)),
             dma((shots - 1,)),
             dma((shots - 1,)),
             dma((max(1, columns - 1), chunk_count)),
@@ -498,7 +539,7 @@
             collective_id=0, has_side_effects=True, vmem_limit_bytes=26 * 2**20),
     )(
         stiffness, buoyancy_first, buoyancy_second, buoyancy_third, adjoint_before[0],
-        adjoint_current[0], forward_field[0], left_halo, right_halo, dense, source_cell[0],
+        adjoint_current[0], forward_field[0], dense, source_cell[0],
     )
     gradient = gradient.reshape(chunk_count, depth, rows // shots, LANES)
     gradient = gradient.transpose(1, 2, 0, 3).reshape(depth, -1)

time: 116 us -> 88.9 us (0.77)
  the two profiles are of different devices: /device:TPU:0 before, /device:TPU:1 now
where the time goes in v4:
time: 88.9 us; the launch traced here: 88.5 us
  Pallas kernels  77.1 us (87%)
  local copies, waits for them, and re-layouts  6.53 us (7%)
  matrix products  2.34 us (3%)
  other arithmetic  1.71 us (2%)
    pallas_call x1, Pallas kernels, local(): pl.pallas_call(functools.partial(wave_body, (steps, depth, rows, chunk_co...  60 us
    pallas_call x1, Pallas kernels, local(): pl.pallas_call(functools.partial(exchange_body, lax.axis_size('shot'), la...  11 us
    pallas_call x1, Pallas kernels, local(): pl.pallas_call(scatter_body, out_shape=jax.ShapeDtypeStruct((chunk_count...  6.06 us
    unnamed x23, local copies, waits for them, and re-layouts  4.64 us

profile of v4, /device:TPU:1, one launch (start us, length us, event | category | flops | bytes accessed | tf_op | source)
XLA Modules:
  0.0 88.5 jit_solution(1970533274743267345)
XLA Ops:
  0.6 0.0 copy-start
  0.7 1.0 %fusion.1 = f32[512]{0:T(512)S(1)} fusion(s32[512]{0:T(512)} %bitcast.38), kind=kOutput, calls=%fused_computation.3 | convolution fusion | flops 17104384 | bytes 4096 | tf_op jit(solution)/shard_map/dot_general | solution.py:451
  1.7 0.7 convert_add_fusion
  2.4 0.7 convert_element_type.22
  3.1 0.0 copy-done
  3.1 0.5 convolution_bitcast_fusion
  3.6 0.8 fusion
  4.4 0.2 reshape.50
  4.6 0.6 reshape.51.mine_ref
  5.2 11.0 %shard_map.130 = f32[32,2,128]{2,1,0:T(2,128)} custom-call(f32[32,2,128]{2,1,0:T(2,128)} %reshape.51.mine_ref), custom_call_target="tpu_custom_call" | custom-call | tf_op jit(solution)/shard_map/pallas_call | solution.py:464
  16.2 0.8 copy.29
  17.0 0.2 reshape.53
  17.2 0.0 copy-start.7
  17.2 0.3 fusion.4
  17.5 0.0 copy-start.6
  17.5 0.1 copy.22
  17.7 0.0 copy-start.1
  17.7 0.0 copy-start.2
  17.7 0.0 copy-start.3
  17.7 0.0 copy-start.4
  17.7 0.0 copy-start.5
  17.7 0.0 copy-start.9
  17.7 6.1 %shard_map.131 = f32[1536,8,128]{2,1,0:T(8,128)S(1)} custom-call(s32[768]{0:T(1024)S(1)} %get-tuple-element.11.row_ref, s32[768]{0:T(1024)S(1)} %get-tuple-element.10.at_ref, s32[768]{0:T(1024)S(1)} %get-tuple-element.9.turn_ref, f32[6,8,128]{2,1,0:T(8,128)S(1)} %bitcast.32), custom_call_target="tpu_custom_call" | custom-call | flops 12582912 | bytes 33554432 | tf_op jit(solution)/shard_map/pallas_call | solution.py:482
  23.8 0.0 copy-done.7
  23.8 0.0 copy-done.6
  23.8 0.0 copy-done.1
  23.8 0.0 copy-done.2
  23.9 0.0 copy-done.3
  23.9 0.0 copy-done.4
  23.9 0.0 copy-done.5
  23.9 0.0 copy-done.9
  23.9 60.0 %shard_map.132 = (f32[3,64,128]{2,1,0:T(8,128)S(1)}, f32[16,32,384]{2,1,0:T(8,128)S(1)}, f32[16,32,384]{2,1,0:T(8,128)S(1)}) custom-call(f32[16,32,384]{2,1,0:T(8,128)S(1)} %copy-done.2, f32[16,32,384]{2,1,0:T(8,128)S(1)} %copy-done.3, f32[16,32,384]{2,1,0:T(8,128)S(1)} %copy-done.4, f32[16,32,384]{2,1,0:T(8,128)S(1)} %copy-done.5, ...), custom_call_target="tpu_custom_call" | custom-call | tf_op jit(solution)/shard_map/pallas_call | solution.py:502
  83.9 0.0 copy-start.8
  84.0 0.9 copy-done.8
  84.8 0.1 copy.28
  84.9 0.7 reshape.57
  85.6 2.1 %copy.32 = f32[1,16,32,384]{3,2,1,0:T(8,128)} copy(f32[1,16,32,384]{3,2,1,0:T(8,128)} %bitcast.31) | data formatting | bytes 1572864
  87.7 0.9 copy.33
  (4 shorter events, 0.1 us)
Async XLA Ops:
  0.6 2.4 %copy-start = (f32[512,256]{1,0:T(8,128)S(1)}, f32[512,256]{1,0:T(8,128)}, u32[]{:S(2)}) copy-start(f32[512,256]{1,0:T(8,128)} %param.18) | copy-start | bytes 1572868
  17.2 6.7 %copy-start.7 = (f32[1,16,32,384]{3,2,1,0:T(8,128)S(1)}, f32[1,16,32,384]{3,2,1,0:T(8,128)}, u32[]{:S(2)}) copy-start(f32[1,16,32,384]{3,2,1,0:T(8,128)} %param.16) | copy-start | bytes 2359300
  17.5 6.4 %copy-start.6 = (f32[1,16,32,384]{3,2,1,0:T(8,128)S(1)}, f32[1,16,32,384]{3,2,1,0:T(8,128)}, u32[]{:S(2)}) copy-start(f32[1,16,32,384]{3,2,1,0:T(8,128)} %param.15) | copy-start | bytes 2359300
  17.7 6.2 %copy-start.1 = (bf16[1,8,16,32,384]{4,3,2,1,0:T(8,128)(2,1)S(1)}, bf16[1,8,16,32,384]{4,3,2,1,0:T(8,128)(2,1)}, u32[]{:S(2)}) copy-start(bf16[1,8,16,32,384]{4,3,2,1,0:T(8,128)(2,1)} %param.17) | copy-start | bytes 9437188
  17.7 6.2 %copy-start.2 = (f32[16,32,384]{2,1,0:T(8,128)S(1)}, f32[16,32,384]{2,1,0:T(8,128)}, u32[]{:S(2)}) copy-start(f32[16,32,384]{2,1,0:T(8,128)} %stiff_hbm.1) | copy-start | bytes 2359300
  17.7 6.2 %copy-start.3 = (f32[16,32,384]{2,1,0:T(8,128)S(1)}, f32[16,32,384]{2,1,0:T(8,128)}, u32[]{:S(2)}) copy-start(f32[16,32,384]{2,1,0:T(8,128)} %first_hbm.1) | copy-start | bytes 2359300
  17.7 6.2 %copy-start.4 = (f32[16,32,384]{2,1,0:T(8,128)S(1)}, f32[16,32,384]{2,1,0:T(8,128)}, u32[]{:S(2)}) copy-start(f32[16,32,384]{2,1,0:T(8,128)} %second_hbm.1) | copy-start | bytes 2359300
  17.7 6.2 %copy-start.5 = (f32[16,32,384]{2,1,0:T(8,128)S(1)}, f32[16,32,384]{2,1,0:T(8,128)}, u32[]{:S(2)}) copy-start(f32[16,32,384]{2,1,0:T(8,128)} %third_hbm.1) | copy-start | bytes 2359300
  17.7 6.2 %copy-start.9 = (s32[1,3]{1,0:T(1,128)S(1)}, s32[1,3]{1,0:T(1,128)}, u32[]{:S(2)}) copy-start(s32[1,3]{1,0:T(1,128)} %param.21) | copy-start | bytes 40
  83.9 0.9 copy-start.8

commit v5 on v4

--- a/solution.py
+++ b/solution.py
@@ -232,7 +232,7 @@
                 * weighted([(near(k), near(1 - k)) for k in range(1, 5)]))
             return inside
 
-        lax.fori_loop(0, tall // 8, out, 0, unroll=8)
+        lax.fori_loop(0, tall // 8, out, 0, unroll=16)
 
         def back(i, inside):
             def near(s):
@@ -241,7 +241,7 @@
                 [(near(k - 1), near(-k)) for k in range(1, 5)])
             return inside
 
-        lax.fori_loop(0, tall // 8, back, 0, unroll=8)
+        lax.fori_loop(0, tall // 8, back, 0, unroll=16)
         for c in range(chunk_count):
             partial[c, pl.ds(g * planes, planes)] = (
                 turned[PAD + c * LANES:PAD + (c + 1) * LANES, :].T.reshape(planes, rows, LANES))
@@ -265,7 +265,7 @@
 
     def inner_all(b):
         lax.fori_loop(0, depth // planes, functools.partial(third_part, b), 0)
-        lax.fori_loop(0, depth, functools.partial(inner_part, b), 0)
+        lax.fori_loop(0, depth, functools.partial(inner_part, b), 0, unroll=2)
 
     for start in (0, PAD + tall):
         turned[start:start + PAD, :] = zero_tile

time: 88.9 us -> 88 us (0.990)
  the two profiles are of different devices: /device:TPU:1 before, /device:TPU:0 now
where the time goes in v5:
time: 88 us; the launch traced here: 86.4 us
  Pallas kernels  75 us (85%)
  local copies, waits for them, and re-layouts  6.53 us (7%)
  matrix products  2.34 us (3%)
  other arithmetic  1.71 us (2%)
    pallas_call x1, Pallas kernels, local(): pl.pallas_call(functools.partial(wave_body, (steps, depth, rows, chunk_co...  57.4 us
    pallas_call x1, Pallas kernels, local(): pl.pallas_call(functools.partial(exchange_body, lax.axis_size('shot'), la...  11.4 us
    pallas_call x1, Pallas kernels, local(): pl.pallas_call(scatter_body, out_shape=jax.ShapeDtypeStruct((chunk_count...  6.15 us
    unnamed x23, local copies, waits for them, and re-layouts  4.64 us

profile of v5, /device:TPU:0, one launch (start us, length us, event | category | flops | bytes accessed | tf_op | source)
XLA Modules:
  0.0 86.4 jit_solution(15325744064850588835)
XLA Ops:
  0.6 0.0 copy-start
  0.7 1.0 %fusion.1 = f32[512]{0:T(512)S(1)} fusion(s32[512]{0:T(512)} %bitcast.38), kind=kOutput, calls=%fused_computation.3 | convolution fusion | flops 17104384 | bytes 4096 | tf_op jit(solution)/shard_map/dot_general | solution.py:451
  1.7 0.7 convert_add_fusion
  2.4 0.7 convert_element_type.22
  3.1 0.0 copy-done
  3.1 0.5 convolution_bitcast_fusion
  3.6 0.8 fusion
  4.4 0.2 reshape.50
  4.6 0.6 reshape.51.mine_ref
  5.2 11.4 %shard_map.130 = f32[32,2,128]{2,1,0:T(2,128)} custom-call(f32[32,2,128]{2,1,0:T(2,128)} %reshape.51.mine_ref), custom_call_target="tpu_custom_call" | custom-call | tf_op jit(solution)/shard_map/pallas_call | solution.py:464
  16.6 0.8 copy.29
  17.3 0.2 reshape.53
  17.5 0.0 copy-start.7
  17.5 0.3 fusion.4
  17.8 0.0 copy-start.6
  17.9 0.1 copy.22
  18.0 0.0 copy-start.1
  18.0 0.0 copy-start.2
  18.1 0.0 copy-start.3
  18.1 0.0 copy-start.4
  18.1 0.0 copy-start.5
  18.1 0.0 copy-start.9
  18.1 6.2 %shard_map.131 = f32[1536,8,128]{2,1,0:T(8,128)S(1)} custom-call(s32[768]{0:T(1024)S(1)} %get-tuple-element.11.row_ref, s32[768]{0:T(1024)S(1)} %get-tuple-element.10.at_ref, s32[768]{0:T(1024)S(1)} %get-tuple-element.9.turn_ref, f32[6,8,128]{2,1,0:T(8,128)S(1)} %bitcast.32), custom_call_target="tpu_custom_call" | custom-call | flops 12582912 | bytes 33554432 | tf_op jit(solution)/shard_map/pallas_call | solution.py:482
  24.3 0.0 copy-done.7
  24.3 0.0 copy-done.6
  24.3 0.0 copy-done.1
  24.3 0.0 copy-done.2
  24.3 0.0 copy-done.3
  24.3 0.0 copy-done.4
  24.3 0.0 copy-done.5
  24.3 0.0 copy-done.9
  24.3 57.4 %shard_map.132 = (f32[3,64,128]{2,1,0:T(8,128)S(1)}, f32[16,32,384]{2,1,0:T(8,128)S(1)}, f32[16,32,384]{2,1,0:T(8,128)S(1)}) custom-call(f32[16,32,384]{2,1,0:T(8,128)S(1)} %copy-done.2, f32[16,32,384]{2,1,0:T(8,128)S(1)} %copy-done.3, f32[16,32,384]{2,1,0:T(8,128)S(1)} %copy-done.4, f32[16,32,384]{2,1,0:T(8,128)S(1)} %copy-done.5, ...), custom_call_target="tpu_custom_call" | custom-call | tf_op jit(solution)/shard_map/pallas_call | solution.py:502
  81.8 0.0 copy-start.8
  81.8 0.9 %copy-done.8 = f32[16,32,384]{2,1,0:T(8,128)} copy-done((f32[16,32,384]{2,1,0:T(8,128)}, f32[16,32,384]{2,1,0:T(8,128)S(1)}, u32[]{:S(2)}) %copy-start.8) | copy-done | bytes 786456
  82.7 0.1 copy.28
  82.7 0.7 reshape.57
  83.4 2.1 %copy.32 = f32[1,16,32,384]{3,2,1,0:T(8,128)} copy(f32[1,16,32,384]{3,2,1,0:T(8,128)} %bitcast.31) | data formatting | bytes 1572864
  85.5 0.9 %copy.33 = f32[1,16,32,384]{3,2,1,0:T(8,128)} copy(f32[1,16,32,384]{3,2,1,0:T(8,128)S(1)} %bitcast.30) | data formatting | bytes 1572864
  (4 shorter events, 0.1 us)
Async XLA Ops:
  0.6 2.4 %copy-start = (f32[512,256]{1,0:T(8,128)S(1)}, f32[512,256]{1,0:T(8,128)}, u32[]{:S(2)}) copy-start(f32[512,256]{1,0:T(8,128)} %param.18) | copy-start | bytes 1572868
  17.5 6.7 %copy-start.7 = (f32[1,16,32,384]{3,2,1,0:T(8,128)S(1)}, f32[1,16,32,384]{3,2,1,0:T(8,128)}, u32[]{:S(2)}) copy-start(f32[1,16,32,384]{3,2,1,0:T(8,128)} %param.16) | copy-start | bytes 2359300
  17.8 6.4 %copy-start.6 = (f32[1,16,32,384]{3,2,1,0:T(8,128)S(1)}, f32[1,16,32,384]{3,2,1,0:T(8,128)}, u32[]{:S(2)}) copy-start(f32[1,16,32,384]{3,2,1,0:T(8,128)} %param.15) | copy-start | bytes 2359300
  18.0 6.2 %copy-start.1 = (bf16[1,8,16,32,384]{4,3,2,1,0:T(8,128)(2,1)S(1)}, bf16[1,8,16,32,384]{4,3,2,1,0:T(8,128)(2,1)}, u32[]{:S(2)}) copy-start(bf16[1,8,16,32,384]{4,3,2,1,0:T(8,128)(2,1)} %param.17) | copy-start | bytes 9437188
  18.0 6.2 %copy-start.2 = (f32[16,32,384]{2,1,0:T(8,128)S(1)}, f32[16,32,384]{2,1,0:T(8,128)}, u32[]{:S(2)}) copy-start(f32[16,32,384]{2,1,0:T(8,128)} %stiff_hbm.1) | copy-start | bytes 2359300
  18.1 6.2 %copy-start.3 = (f32[16,32,384]{2,1,0:T(8,128)S(1)}, f32[16,32,384]{2,1,0:T(8,128)}, u32[]{:S(2)}) copy-start(f32[16,32,384]{2,1,0:T(8,128)} %first_hbm.1) | copy-start | bytes 2359300
  18.1 6.2 %copy-start.4 = (f32[16,32,384]{2,1,0:T(8,128)S(1)}, f32[16,32,384]{2,1,0:T(8,128)}, u32[]{:S(2)}) copy-start(f32[16,32,384]{2,1,0:T(8,128)} %second_hbm.1) | copy-start | bytes 2359300
  18.1 6.2 %copy-start.5 = (f32[16,32,384]{2,1,0:T(8,128)S(1)}, f32[16,32,384]{2,1,0:T(8,128)}, u32[]{:S(2)}) copy-start(f32[16,32,384]{2,1,0:T(8,128)} %third_hbm.1) | copy-start | bytes 2359300
  18.1 6.2 %copy-start.9 = (s32[1,3]{1,0:T(1,128)S(1)}, s32[1,3]{1,0:T(1,128)}, u32[]{:S(2)}) copy-start(s32[1,3]{1,0:T(1,128)} %param.21) | copy-start | bytes 40
  81.8 0.9 %copy-start.8 = (f32[16,32,384]{2,1,0:T(8,128)}, f32[16,32,384]{2,1,0:T(8,128)S(1)}, u32[]{:S(2)}) copy-start(f32[16,32,384]{2,1,0:T(8,128)S(1)} %get-tuple-element.7) | copy-start | bytes 2359300
